TPU v7x, 512 devices: a whole 4x8x8 slice. The times are simulated.
512 devices in a mesh: dp: 32 (over x, z), hid: 16 (over y, core).
Axes of the slice: x: 4, y: 8, z: 8, core: 2. Of those that a mesh axis runs over, the one named last changes fastest.
Arguments:
- inputs: bfloat16 [8192, 8192], P('dp', 'hid'), may hold values from -6 to 6
- out_grad: bfloat16 [8192, 8192], P('dp', 'hid'), may hold values from -6 to 6
- home_block: int32 [64], P('hid'), may hold values from 0 to 1
- blocks_up: bfloat16 [64, 3, 256, 256], P('hid', None, 'dp'), may hold values from -0.21875 to 0.21875
- blocks_down: bfloat16 [64, 3, 256, 256], P('hid', None, 'dp'), may hold values from -0.15625 to 0.15625
- up_left: bfloat16 [8192, 128], P('hid', 'dp'), may hold values from -0.0625 to 0.0625
- up_right: bfloat16 [128, 16384], P('dp', 'hid'), may hold values from -0.5 to 0.5
- down_left: bfloat16 [16384, 128], P('hid', 'dp'), may hold values from -0.046875 to 0.046875
- down_right: bfloat16 [128, 8192], P('dp', 'hid'), may hold values from -0.5 to 0.5
Outputs:
- outputs: bfloat16 [8192, 8192], P('dp', 'hid')
- input_grad: bfloat16 [8192, 8192], P('dp', 'hid')
- grad_blocks_up: bfloat16 [64, 3, 256, 256], P('hid', None, 'dp')
- grad_blocks_down: bfloat16 [64, 3, 256, 256], P('hid', None, 'dp')
- grad_up_left: bfloat16 [8192, 128], P('hid', 'dp')
- grad_up_right: bfloat16 [128, 16384], P('dp', 'hid')
- grad_down_left: bfloat16 [16384, 128], P('hid', 'dp')
- grad_down_right: bfloat16 [128, 8192], P('dp', 'hid')
All inputs are finite; a program needn't handle non-finite values.
Results may differ from a plain program's by a relative error of at most 0.022.
Values may be sent and summed in bfloat16 or wider, within the bound.
A program may use at most 64 MiB of HBM per device.

v0:
```python
import jax
import jax.numpy as jnp
from jax import lax
from jax.sharding import PartitionSpec as P

gelu_coef = 0.7978845608028654
cubic_coef = 0.044715


def from_partner(value, axis, distance):
    mask = 2**distance
    pairs = [(source, source ^ mask) for source in range(lax.axis_size(axis))]
    return lax.ppermute(value, axis, pairs)


def gelu_pair(pre_act):
    tangent = jnp.tanh(gelu_coef * (pre_act + cubic_coef * pre_act * pre_act * pre_act))
    activated = 0.5 * pre_act * (1.0 + tangent)
    derivative = 0.5 * (1.0 + tangent) + 0.5 * pre_act * (1.0 - tangent * tangent) * gelu_coef * (
        1.0 + 3.0 * cubic_coef * pre_act * pre_act
    )
    return (activated, derivative)


def per_device(
    inputs, out_grad, home_block, blocks_up, blocks_down, up_left, up_right, down_left, down_right
):
    single = jnp.float32
    half_type = jnp.bfloat16
    highest = lax.Precision.HIGHEST
    row_count, width_dev = inputs.shape
    hid_blocks, slot_count, shard_rows, blk_size = blocks_up.shape
    level_count = slot_count - 1
    in_blocks = width_dev // blk_size
    hidden_dev = hid_blocks * blk_size
    top_bit = lax.axis_size("hid").bit_length() - 1
    grad_scale = float(lax.axis_size("dp") * row_count) ** (-0.5)
    select = (home_block[:, None] == jnp.arange(in_blocks, dtype=jnp.int32)[None, :]).astype(single)
    full_up, full_down, left_in, right_in, left_out, right_out = (
        lax.all_gather(blocks_up, "dp", axis=2, tiled=True),
        lax.all_gather(blocks_down, "dp", axis=2, tiled=True),
        lax.all_gather(up_left, "dp", axis=1, tiled=True),
        lax.all_gather(up_right, "dp", axis=0, tiled=True),
        lax.all_gather(down_left, "dp", axis=1, tiled=True),
        lax.all_gather(down_right, "dp", axis=0, tiled=True),
    )
    rank_in = lax.psum(jnp.dot(inputs, left_in, preferred_element_type=single), "hid")
    rank_in = rank_in.astype(half_type)
    in_pieces = [inputs]
    grad_pieces = [out_grad]
    for level_idx in range(level_count):
        in_pieces.append(from_partner(inputs, "hid", top_bit - 1 - level_idx))

    def pick_blocks(pieces):
        stacked = jnp.stack(pieces, 0).reshape(slot_count, row_count, in_blocks, blk_size)
        return jnp.take(stacked, home_block, axis=2)

    picked = pick_blocks(in_pieces)
    part_rows = picked
    up_sum = jnp.einsum("sthk,hskn->thn", part_rows, full_up, preferred_element_type=single)
    pre_act = up_sum.reshape(row_count, hidden_dev) + jnp.dot(
        rank_in, right_in, preferred_element_type=single
    )
    activated, derivative = gelu_pair(pre_act)
    hidden = activated.astype(half_type)
    hidden_blocks = hidden.reshape(row_count, hid_blocks, blk_size)
    rank_mid = lax.psum(jnp.dot(hidden, left_out, preferred_element_type=single), "hid").astype(
        half_type
    )
    part_rows = hidden_blocks
    down_sum = jnp.einsum("thk,hskn->sthn", part_rows, full_down, preferred_element_type=single)
    placed = jnp.einsum("sthn,hi->stin", down_sum, select, precision=highest)
    total = placed[0]
    for level_idx in range(level_count):
        arrived = from_partner(placed[level_idx + 1], "hid", top_bit - 1 - level_idx)
        total = total + arrived
    outputs = (
        total.reshape(row_count, width_dev)
        + jnp.dot(rank_mid, right_out, preferred_element_type=single)
    ).astype(half_type)
    rank_back = lax.psum(jnp.dot(out_grad, right_out.T, preferred_element_type=single), "hid")
    rank_back = rank_back.astype(half_type)
    for level_idx in range(level_count):
        grad_pieces.append(from_partner(out_grad, "hid", top_bit - 1 - level_idx))
    grad_picked = pick_blocks(grad_pieces)
    grad_hidden = jnp.einsum(
        "sthn,hskn->thk", grad_picked, full_down, preferred_element_type=single
    )
    grad_pre = (
        (
            grad_hidden.reshape(row_count, hidden_dev)
            + jnp.dot(rank_back, left_out.T, preferred_element_type=single)
        )
        * derivative
    ).astype(half_type)
    rank_grad = lax.psum(
        jnp.dot(grad_pre, right_in.T, preferred_element_type=single), "hid"
    ).astype(half_type)
    grad_blocks = grad_pre.reshape(row_count, hid_blocks, blk_size)
    back_sum = jnp.einsum("thn,hskn->sthk", grad_blocks, full_up, preferred_element_type=single)
    back_placed = jnp.einsum("sthk,hi->stik", back_sum, select, precision=highest)
    back_total = back_placed[0]
    for level_idx in range(level_count):
        arrived = from_partner(back_placed[level_idx + 1], "hid", top_bit - 1 - level_idx)
        back_total = back_total + arrived
    input_grad = (
        back_total.reshape(row_count, width_dev)
        + jnp.dot(rank_grad, left_in.T, preferred_element_type=single)
    ).astype(half_type)
    summed = (
        lax.psum_scatter(
            (
                grad_scale
                * jnp.einsum("sthk,thn->hskn", picked, grad_blocks, preferred_element_type=single)
            ).astype(jnp.bfloat16),
            "dp",
            scatter_dimension=2,
            tiled=True,
        ).astype(jnp.float32),
        lax.psum_scatter(
            (
                grad_scale
                * jnp.einsum(
                    "thk,sthn->hskn", hidden_blocks, grad_picked, preferred_element_type=single
                )
            ).astype(jnp.bfloat16),
            "dp",
            scatter_dimension=2,
            tiled=True,
        ).astype(jnp.float32),
        lax.psum_scatter(
            (grad_scale * jnp.dot(inputs.T, rank_grad, preferred_element_type=single)).astype(
                jnp.bfloat16
            ),
            "dp",
            scatter_dimension=1,
            tiled=True,
        ).astype(jnp.float32),
        lax.psum_scatter(
            (grad_scale * jnp.dot(rank_in.T, grad_pre, preferred_element_type=single)).astype(
                jnp.bfloat16
            ),
            "dp",
            scatter_dimension=0,
            tiled=True,
        ).astype(jnp.float32),
        lax.psum_scatter(
            (grad_scale * jnp.dot(hidden.T, rank_back, preferred_element_type=single)).astype(
                jnp.bfloat16
            ),
            "dp",
            scatter_dimension=1,
            tiled=True,
        ).astype(jnp.float32),
        lax.psum_scatter(
            (grad_scale * jnp.dot(rank_mid.T, out_grad, preferred_element_type=single)).astype(
                jnp.bfloat16
            ),
            "dp",
            scatter_dimension=0,
            tiled=True,
        ).astype(jnp.float32),
    )
    return (outputs, input_grad) + tuple((summed_part.astype(half_type) for summed_part in summed))


def solution(mesh):
    placed = (
        P("dp", "hid"),
        P("dp", "hid"),
        P("hid"),
        P("hid", None, "dp", None),
        P("hid", None, "dp", None),
        P("hid", "dp"),
        P("dp", "hid"),
        P("hid", "dp"),
        P("dp", "hid"),
    )
    return jax.shard_map(
        per_device,
        mesh=mesh,
        in_specs=placed,
        out_specs=(
            P("dp", "hid"),
            P("dp", "hid"),
            P("hid", None, "dp", None),
            P("hid", None, "dp", None),
            P("hid", "dp"),
            P("dp", "hid"),
            P("hid", "dp"),
            P("dp", "hid"),
        ),
        check_vma=False,
    )
```

profile of v0, /device:TPU:1, one launch (start us, length us, event | category | flops | bytes accessed | tf_op | source)
XLA Modules:
  0.0 734.4 jit_solution(1994460682840392459)
XLA Ops:
  8.7 1.1 copy.54
  9.8 8.3 %collective-permute-start = (bf16[256,512]{0,1:T(8,128)(2,1)S(1)}, bf16[256,512]{0,1:T(8,128)(2,1)S(1)}, u32[]{:S(2)}, u32[]{:S(2)}) collective-permute-start(bf16[256,512]{0,1:T(8,128)(2,1)S(1)} %copy.54), channel_id=1, source_target_pairs={{0,8},{1,9},{2,10},{3,11},{4,12},{5,13},{6,14},{7,15},{8,0},{9,1},... | collective-permute-start | bytes 786440 | tf_op jit(solution)/shard_map/ppermute | solution.py:13
  18.1 2.4 collective-permute-start.1
  20.6 1.1 copy.63
  21.6 3.5 collective-permute-start.4
  25.2 2.1 collective-permute-start.5
  27.5 41.8 %all-gather = bf16[32,4,512]{2,1,0:T(4,128)(2,1)S(1)} all-gather(bf16[1,4,512]{2,1,0:T(4,128)(2,1)S(1)} %bitcast.138), channel_id=1, replica_groups=mesh['dp'=32,'hid'=16] {'dp'}, dimensions={0}, use_global_device_ids=true | all-gather | bytes 135168 | tf_op jit(solution)/shard_map/all_gather | solution.py:42
  69.6 33.8 %all-gather.3 = bf16[32,4,512]{2,1,0:T(4,128)(2,1)S(1)} all-gather(bf16[1,4,512]{2,1,0:T(4,128)(2,1)S(1)} %bitcast.139), channel_id=1, replica_groups=mesh['dp'=32,'hid'=16] {'dp'}, dimensions={0}, use_global_device_ids=true | all-gather | bytes 135168 | tf_op jit(solution)/shard_map/all_gather | solution.py:45
  103.7 36.1 %all-gather.1 = bf16[32,4,1024]{2,1,0:T(4,128)(2,1)S(1)} all-gather(bf16[1,4,1024]{2,1,0:T(4,128)(2,1)S(1)} %bitcast.136), channel_id=1, replica_groups=mesh['dp'=32,'hid'=16] {'dp'}, dimensions={0}, use_global_device_ids=true | all-gather | bytes 270336 | tf_op jit(solution)/shard_map/all_gather | solution.py:43
  139.9 0.8 copy.66
  140.8 73.3 %all-reduce.13 = (bf16[256,128]{1,0:T(8,128)(2,1)S(1)}, bf16[256,128]{1,0:T(8,128)(2,1)S(1)}) all-reduce(f32[256,128]{1,0:T(8,128)S(1)} %fusion.57, f32[256,128]{1,0:T(8,128)S(1)} %fusion.59), channel_id=1, replica_groups=mesh['dp'=32,'hid'=16] {'hid'}, use_global_device_ids=true, to_apply=%region_0.2 | all-reduce | flops 65536 | bytes 393216 | tf_op jit(solution)/shard_map/psum | solution.py:47
  214.1 36.0 %all-gather.2 = bf16[32,4,1024]{2,1,0:T(4,128)(2,1)S(1)} all-gather(bf16[1,4,1024]{2,1,0:T(4,128)(2,1)S(1)} %bitcast.137), channel_id=1, replica_groups=mesh['dp'=32,'hid'=16] {'dp'}, dimensions={0}, use_global_device_ids=true | all-gather | bytes 270336 | tf_op jit(solution)/shard_map/all_gather | solution.py:44
  251.2 0.8 copy.67
  253.7 1.8 pad_maximum_fusion.1
  255.4 1.9 gather_fusion.1
  257.3 3.2 fusion.8
  260.5 2.6 copy.60
  263.2 3.1 fusion.5
  266.3 2.7 copy.89
  271.4 1.0 fusion.21
  273.1 1.0 fusion.22
  274.0 60.1 %all-reduce.14 = (bf16[256,128]{1,0:T(8,128)(2,1)S(1)}, bf16[256,128]{1,0:T(8,128)(2,1)S(1)}) all-reduce(f32[256,128]{1,0:T(8,128)S(1)} %fusion.58, f32[256,128]{1,0:T(8,128)S(1)} %fusion.60), channel_id=1, replica_groups=mesh['dp'=32,'hid'=16] {'hid'}, use_global_device_ids=true, to_apply=%region_1.0 | all-reduce | flops 65536 | bytes 393216 | tf_op jit(solution)/shard_map/psum | solution.py:67
  334.1 0.9 fusion.24
  335.0 0.9 fusion.25
  335.9 2.3 fusion.10
  338.1 2.4 copy.76
  340.8 1.4 dynamic-slice
  343.8 0.9 multiply_convert_fusion.1
  344.7 1.4 copy.117
  346.1 2.9 reshape.97
  349.0 1.4 copy-done.3
  351.0 4.1 fusion.16
  355.4 7.4 %collective-permute-start.6 = (f32[256,2,256]{2,1,0:T(2,128)S(1)}, f32[256,2,256]{2,1,0:T(2,128)S(1)}, u32[]{:S(2)}, u32[]{:S(2)}) collective-permute-start(f32[256,2,256]{2,1,0:T(2,128)S(1)} %get-tuple-element.50), channel_id=1, source_target_pairs={{0,8},{1,9},{2,10},{3,11},{4,12},{5,13},{6,14},{7,15},{8,0},{9,1},... | collective-permute-start | bytes 1572872 | tf_op jit(solution)/shard_map/ppermute | solution.py:13
  362.9 1.9 collective-permute-start.7
  365.4 4.1 fusion.13
  369.8 5.1 collective-permute-start.2
  374.9 1.9 collective-permute-start.3
  377.3 19.0 %collective-permute-done.6 = f32[256,2,256]{2,1,0:T(2,128)S(1)} collective-permute-done((f32[256,2,256]{2,1,0:T(2,128)S(1)}, f32[256,2,256]{2,1,0:T(2,128)S(1)}, u32[]{:S(2)}, u32[]{:S(2)}) %collective-permute-start.6) | collective-permute-done | bytes 524320 | tf_op jit(solution)/shard_map/ppermute | solution.py:13
  396.3 46.2 %collective-permute-done.7 = f32[256,2,256]{2,1,0:T(2,128)S(1)} collective-permute-done((f32[256,2,256]{2,1,0:T(2,128)S(1)}, f32[256,2,256]{2,1,0:T(2,128)S(1)}, u32[]{:S(2)}, u32[]{:S(2)}) %collective-permute-start.7) | collective-permute-done | bytes 524320 | tf_op jit(solution)/shard_map/ppermute | solution.py:13
  442.9 10.8 %collective-permute-done.3 = f32[256,2,256]{2,1,0:T(2,128)S(1)} collective-permute-done((f32[256,2,256]{2,1,0:T(2,128)S(1)}, f32[256,2,256]{2,1,0:T(2,128)S(1)}, u32[]{:S(2)}, u32[]{:S(2)}) %collective-permute-start.3) | collective-permute-done | bytes 524320 | tf_op jit(solution)/shard_map/ppermute | solution.py:13
  454.1 0.9 add_convert_fusion
  455.1 47.8 %all-reduce.12.cloned.1.call-done = (bf16[4,3,256,256]{3,0,1,2:T(4,128)(2,1)}, bf16[512,128]{0,1:T(8,128)(2,1)}, bf16[128,1024]{1,0:T(8,128)(2,1)}, bf16[1024,128]{0,1:T(8,128)(2,1)}, bf16[128,512]{1,0:T(8,128)(2,1)}) async-done(((bf16[4,3,256,256]{3,0,1,2:T(4,128)(2,1)}, bf16[512,128]{0,1:T(8,128)(2,1)}, bf16[128,1024]{1,0:T(8,128)(2,1)}, bf16[1024,128]{0,1:T(8,128)(2,1)}, bf16[128,512]{1,0:T(8,128)(2,1)}), ...) | async-done | bytes 2359312
  504.3 1.3 constant_dynamic-slice_fusion
  505.6 1.3 constant_dynamic-slice_fusion.3
  506.9 1.3 constant_dynamic-slice_fusion.1
  508.2 1.3 constant_dynamic-slice_fusion.2
  509.5 216.8 %reduce-scatter.4.cloned.1.call-done = bf16[8,3072]{1,0:T(8,128)(2,1)} async-done(((bf16[256,3072]{1,0:T(8,128)(2,1)}), bf16[8,3072]{1,0:T(8,128)(2,1)}) %reduce-scatter.4.cloned.1.call-update) | async-done | bytes 49168
  726.3 0.9 reshape.98
  (78 shorter events, 13.8 us)
Async XLA Ops:
  7.2 62.2 %copy-start.2 = (bf16[256,512]{1,0:T(8,128)(2,1)S(1)}, bf16[256,512]{1,0:T(8,128)(2,1)}, u32[]{:S(2)}) copy-start(bf16[256,512]{1,0:T(8,128)(2,1)} %param.11) | copy-start | bytes 786436
  7.2 96.3 %copy-start.1 = (bf16[256,512]{1,0:T(8,128)(2,1)S(1)}, bf16[256,512]{1,0:T(8,128)(2,1)}, u32[]{:S(2)}) copy-start(bf16[256,512]{1,0:T(8,128)(2,1)} %param.12) | copy-start | bytes 786436
  7.2 20.3 %copy-start.12 = (bf16[512,4]{0,1:T(4,128)(2,1)S(1)}, bf16[512,4]{0,1:T(4,128)(2,1)}, u32[]{:S(2)}) copy-start(bf16[512,4]{0,1:T(4,128)(2,1)} %param.16) | copy-start | bytes 12292
  7.2 62.4 %copy-start.13 = (bf16[4,512]{1,0:T(4,128)(2,1)S(1)}, bf16[4,512]{1,0:T(4,128)(2,1)}, u32[]{:S(2)}) copy-start(bf16[4,512]{1,0:T(4,128)(2,1)} %param.19) | copy-start | bytes 12292
  7.2 250.1 %all-gather.7.cloned.1.call-start = ((), (), s32[]{:S(2)}) async-start(), calls=%async_computation.1 | async-start | bytes 1622016 | tf_op jit(solution)/shard_map/all_gather | solution.py:40
  7.9 255.2 %all-gather.9.cloned.1.call-start = ((), (), s32[]{:S(2)}) async-start(), calls=%async_computation.2 | async-start | bytes 1622016 | tf_op jit(solution)/shard_map/all_gather | solution.py:41
  8.7 494.1 %all-reduce.12.cloned.1.call-start = ((), (), s32[]{:S(2)}) async-start(), calls=%async_computation.4 | async-start | bytes 4718592
  9.8 93.9 %copy-start.10 = (bf16[4,1024]{1,0:T(4,128)(2,1)S(1)}, bf16[4,1024]{1,0:T(4,128)(2,1)}, u32[]{:S(2)}) copy-start(bf16[4,1024]{1,0:T(4,128)(2,1)} %param.17) | copy-start | bytes 24580
  9.8 241.1 %collective-permute-start = (bf16[256,512]{0,1:T(8,128)(2,1)S(1)}, bf16[256,512]{0,1:T(8,128)(2,1)S(1)}, u32[]{:S(2)}, u32[]{:S(2)}) collective-permute-start(bf16[256,512]{0,1:T(8,128)(2,1)S(1)} %copy.54), channel_id=1, source_target_pairs={{0,8},{1,9},{2,10},{3,11},{4,12},{5,13},{6,14},{7,15},{8,0},{9,1},... | collective-permute-start | bytes 786440 | tf_op jit(solution)/shard_map/ppermute | solution.py:13
  18.1 232.9 %collective-permute-start.1 = (bf16[256,512]{0,1:T(8,128)(2,1)S(1)}, bf16[256,512]{0,1:T(8,128)(2,1)S(1)}, u32[]{:S(2)}, u32[]{:S(2)}) collective-permute-start(bf16[256,512]{0,1:T(8,128)(2,1)S(1)} %copy.54), channel_id=1, source_target_pairs={{0,4},{1,5},{2,6},{3,7},{4,0},{5,1},{6,2},{7,3},{8,12},{9,13},{10,... | collective-permute-start | bytes 786440 | tf_op jit(solution)/shard_map/ppermute | solution.py:13
  21.6 229.6 %collective-permute-start.4 = (bf16[256,512]{0,1:T(8,128)(2,1)S(1)}, bf16[256,512]{0,1:T(8,128)(2,1)S(1)}, u32[]{:S(2)}, u32[]{:S(2)}) collective-permute-start(bf16[256,512]{0,1:T(8,128)(2,1)S(1)} %copy.63), channel_id=1, source_target_pairs={{0,8},{1,9},{2,10},{3,11},{4,12},{5,13},{6,14},{7,15},{8,0},{9,1},... | collective-permute-start | bytes 786440 | tf_op jit(solution)/shard_map/ppermute | solution.py:13
  25.2 226.9 %collective-permute-start.5 = (bf16[256,512]{0,1:T(8,128)(2,1)S(1)}, bf16[256,512]{0,1:T(8,128)(2,1)S(1)}, u32[]{:S(2)}, u32[]{:S(2)}) collective-permute-start(bf16[256,512]{0,1:T(8,128)(2,1)S(1)} %copy.63), channel_id=1, source_target_pairs={{0,4},{1,5},{2,6},{3,7},{4,0},{5,1},{6,2},{7,3},{8,12},{9,13},{10,... | collective-permute-start | bytes 786440 | tf_op jit(solution)/shard_map/ppermute | solution.py:13
  27.5 113.3 %copy-start.14 = (s32[4]{0:T(128)S(1)}, s32[4]{0:T(128)}, u32[]{:S(2)}) copy-start(s32[4]{0:T(128)} %param.13) | copy-start | bytes 52
  69.4 144.7 %copy-start.11 = (bf16[1024,4]{0,1:T(4,128)(2,1)S(1)}, bf16[1024,4]{0,1:T(4,128)(2,1)}, u32[]{:S(2)}) copy-start(bf16[1024,4]{0,1:T(4,128)(2,1)} %param.18) | copy-start | bytes 24580
  253.7 3.6 copy-start.4
  260.5 2.7 copy-start.6
  266.3 2.7 copy-start.8
  269.0 0.9 copy-start.7
  269.0 1.3 copy-start.9
  340.5 3.3 copy-start.5
  340.5 385.8 %reduce-scatter.4.cloned.1.call-start = ((), (), s32[]{:S(2)}) async-start(), calls=%async_computation.3 | async-start | bytes 1622016
  349.0 1.4 copy-start.3
  355.1 9.7 %copy-start = (bf16[4,3,256,256]{3,2,1,0:T(8,128)(2,1)S(1)}, bf16[4,3,256,256]{3,2,1,0:T(8,128)(2,1)}, u32[]{:S(2)}) copy-start(bf16[4,3,256,256]{3,2,1,0:T(8,128)(2,1)} %all-gather.9.cloned.1.call-done) | copy-start | bytes 4718596
  355.4 40.9 %collective-permute-start.6 = (f32[256,2,256]{2,1,0:T(2,128)S(1)}, f32[256,2,256]{2,1,0:T(2,128)S(1)}, u32[]{:S(2)}, u32[]{:S(2)}) collective-permute-start(f32[256,2,256]{2,1,0:T(2,128)S(1)} %get-tuple-element.50), channel_id=1, source_target_pairs={{0,8},{1,9},{2,10},{3,11},{4,12},{5,13},{6,14},{7,15},{8,0},{9,1},... | collective-permute-start | bytes 1572872 | tf_op jit(solution)/shard_map/ppermute | solution.py:13
  362.9 79.6 %collective-permute-start.7 = (f32[256,2,256]{2,1,0:T(2,128)S(1)}, f32[256,2,256]{2,1,0:T(2,128)S(1)}, u32[]{:S(2)}, u32[]{:S(2)}) collective-permute-start(f32[256,2,256]{2,1,0:T(2,128)S(1)} %get-tuple-element.51), channel_id=1, source_target_pairs={{0,4},{1,5},{2,6},{3,7},{4,0},{5,1},{6,2},{7,3},{8,12},{9,13},{10,... | collective-permute-start | bytes 1572872 | tf_op jit(solution)/shard_map/ppermute | solution.py:13
  369.8 73.1 %collective-permute-start.2 = (f32[256,2,256]{2,1,0:T(2,128)S(1)}, f32[256,2,256]{2,1,0:T(2,128)S(1)}, u32[]{:S(2)}, u32[]{:S(2)}) collective-permute-start(f32[256,2,256]{2,1,0:T(2,128)S(1)} %get-tuple-element.52), channel_id=1, source_target_pairs={{0,8},{1,9},{2,10},{3,11},{4,12},{5,13},{6,14},{7,15},{8,0},{9,1},... | collective-permute-start | bytes 1572872 | tf_op jit(solution)/shard_map/ppermute | solution.py:13
  374.9 78.8 %collective-permute-start.3 = (f32[256,2,256]{2,1,0:T(2,128)S(1)}, f32[256,2,256]{2,1,0:T(2,128)S(1)}, u32[]{:S(2)}, u32[]{:S(2)}) collective-permute-start(f32[256,2,256]{2,1,0:T(2,128)S(1)} %get-tuple-element.53), channel_id=1, source_target_pairs={{0,4},{1,5},{2,6},{3,7},{4,0},{5,1},{6,2},{7,3},{8,12},{9,13},{10,... | collective-permute-start | bytes 1572872 | tf_op jit(solution)/shard_map/ppermute | solution.py:13
Sparse Core Ops, SparseCore 0:
  11.1 81.0 all-gather.6
  95.3 77.8 all-gather.8
  340.6 162.1 all-reduce.11
  507.7 218.5 reduce-scatter.3
where the time goes:
time: 740 us; the launch traced here: 734 us
  waiting for transfers between devices  342 us (46%)
  blocking collectives  281 us (38%)
  local copies, waits for them, and re-layouts  33.8 us (5%)
  starting transfers between devices  33 us (4%)
  matrix products  25.2 us (3%)
  between operations  15.5 us (2%)
    unnamed x6, waiting for transfers between devices  266 us
    ppermute x8, waiting for transfers between devices, from_partner(): return lax.ppermute(value, axis, pairs)  76 us
    psum x1, blocking collectives, per_device(): lax.psum(jnp.dot(inputs, left_in, preferred_element_type=single), 'hid')  73.3 us
    psum x1, blocking collectives, per_device(): lax.psum(jnp.dot(hidden, left_out, preferred_element_type=single), 'hid')  60.1 us
    all_gather x1, blocking collectives, per_device(): lax.all_gather(up_left, 'dp', axis=1, tiled=True)  41.8 us
    all_gather x1, blocking collectives, per_device(): lax.all_gather(up_right, 'dp', axis=0, tiled=True)  36.1 us
    all_gather x1, blocking collectives, per_device(): lax.all_gather(down_left, 'dp', axis=1, tiled=True)  36 us
    all_gather x1, blocking collectives, per_device(): lax.all_gather(down_right, 'dp', axis=0, tiled=True)  33.8 us
  transfers between devices with their start and end apart: 12, of which 5 were waited for; matrix products, arithmetic and copies ran while one was open for 6% of the time, Pallas kernels for 0%

commit v1 on v0

v1 whole, which is shorter than its diff:
```python
import functools

import jax
import jax.numpy as jnp
from jax import lax
from jax.experimental import pallas as pl
from jax.experimental.pallas import tpu as pltpu
from jax.sharding import PartitionSpec as P

MESH = pl.DeviceIdType.MESH
gelu_coef = 0.7978845608028654
cubic_coef = 0.044715
SLOTS = 3
F32 = jnp.float32
BF16 = jnp.bfloat16
NN = (((1,), (0,)), ((), ()))
NT = (((1,), (1,)), ((), ()))


def dot(a, b, dims=NN):
    return lax.dot_general(a, b, dims, preferred_element_type=F32)


def flip(index, bit):
    return index + bit - 2 * bit * lax.rem(lax.div(index, bit), 2)


def wrap(value, n):
    return lax.rem(value + 4 * n, n)


def gelu_pair(pre_act):
    tangent = jnp.tanh(gelu_coef * (pre_act + cubic_coef * pre_act * pre_act * pre_act))
    activated = 0.5 * pre_act * (1.0 + tangent)
    derivative = 0.5 * (1.0 + tangent) + 0.5 * pre_act * (1.0 - tangent * tangent) * gelu_coef * (
        1.0 + 3.0 * cubic_coef * pre_act * pre_act
    )
    return activated, derivative


class Place:
    def __init__(self, nx, nz, nh):
        self.size = {"x": nx, "z": nz}
        self.nh = nh
        self.dp = lax.axis_index("dp")
        self.hid = lax.axis_index("hid")
        self.pos = {"x": lax.div(self.dp, nz), "z": lax.rem(self.dp, nz)}
        self.near = (self.dp, flip(self.hid, nh // 4))
        self.far = (self.dp, flip(flip(self.hid, nh // 4), nh // 2))

    def neighbour(self, axis, o):
        x, z = self.pos["x"], self.pos["z"]
        if axis == "x":
            x = wrap(x + o, self.size["x"])
        else:
            z = wrap(z + o, self.size["z"])
        return (x * self.size["z"] + z, self.hid)

    def peer(self, j):
        return (self.dp, lax.rem(self.hid + j, self.nh))


def gather_axes(kind):
    return ("x", "z") if kind < 2 else ("z", "x")


def ring_dirs(n):
    return [(0, n // 2)] + ([(1, n // 2 - 1)] if n > 2 else [])


class Gather:
    def __init__(self, place, buf, kind, width, send_sem, recv_sem):
        self.place, self.buf, self.kind = place, buf, kind
        self.columns = pl.ds(kind * width, width)
        self.send_sem, self.recv_sem = send_sem, recv_sem
        self.axes = gather_axes(kind)
        self.turns = [place.size[a] // 2 for a in self.axes]
        self.rounds = sum(self.turns)
        self.sent = {}

    def part(self, phase, at):
        axis = self.axes[phase]
        own = self.place.pos
        if phase == 0:
            x, z = (at, own["z"]) if axis == "x" else (own["x"], at)
            return self.buf.at[x, z, :, self.columns]
        if axis == "x":
            return self.buf.at[at, :, :, self.columns]
        return self.buf.at[:, at, :, self.columns]

    def copy(self, phase, d, t, at):
        axis = self.axes[phase]
        o = (1 if self.kind % 2 == 0 else -1) * (1 if d == 0 else -1)
        n = self.place.size[axis]
        first = 0 if phase == 0 else self.place.size[self.axes[0]] - 1
        slot = first + (n // 2 if d else 0) + t - 1
        ref = self.part(phase, wrap(self.place.pos[axis] - o * at, n))
        return pltpu.make_async_remote_copy(
            src_ref=ref,
            dst_ref=ref,
            send_sem=self.send_sem.at[self.kind, phase * 2 + d],
            recv_sem=self.recv_sem.at[self.kind, slot],
            device_id=self.place.neighbour(axis, o),
            device_id_type=MESH,
        )

    def send(self, phase, d, t):
        before = self.sent.pop((phase, d), None)
        if before is not None:
            before.wait_send()
        made = self.copy(phase, d, t, t - 1)
        made.start()
        self.sent[(phase, d)] = made

    def begin(self, phase):
        for d, count in ring_dirs(self.place.size[self.axes[phase]]):
            self.send(phase, d, 1)

    def advance(self, k):
        if k == 0:
            self.begin(0)
            return
        phase = 0 if k <= self.turns[0] else 1
        t = k - (self.turns[0] if phase else 0)
        for d, count in ring_dirs(self.place.size[self.axes[phase]]):
            if t <= count:
                self.copy(phase, d, t, t).wait_recv()
                if t < count:
                    self.send(phase, d, t + 1)
        if phase == 0 and t == self.turns[0]:
            self.begin(1)

    def finish(self):
        for made in self.sent.values():
            made.wait_send()
        self.sent = {}


class Scatter:
    def __init__(self, place, terms, kind, width, first_buf, second_buf, send_sem, recv_sem):
        self.place, self.terms, self.kind = place, terms, kind
        self.columns = pl.ds(kind * width, width)
        self.bufs = (first_buf, second_buf)
        self.send_sem, self.recv_sem = send_sem, recv_sem
        self.axes = gather_axes(kind)[::-1]
        self.turns = [place.size[a] // 2 for a in self.axes]
        self.rounds = sum(self.turns)
        self.sent = {}

    def term(self, phase, at):
        axis = self.axes[phase]
        own = self.place.pos
        if phase == 1:
            x, z = (at, own["z"]) if axis == "x" else (own["x"], at)
            return self.terms.at[x, z, :, self.columns]
        if axis == "x":
            return self.terms.at[at, :, :, self.columns]
        return self.terms.at[:, at, :, self.columns]

    def slot(self, phase, d, t):
        n = self.place.size[self.axes[phase]]
        return (n // 2 if d else 0) + t - 1

    def arrived(self, phase, d, t):
        return self.bufs[phase].at[self.kind % 2, self.slot(phase, d, t)]

    def o(self, d):
        return (1 if self.kind % 2 == 0 else -1) * (1 if d == 0 else -1)

    def copy(self, phase, d, t, source):
        axis = self.axes[phase]
        first = 0 if phase == 0 else self.place.size[self.axes[0]] - 1
        return pltpu.make_async_remote_copy(
            src_ref=source,
            dst_ref=self.arrived(phase, d, t),
            send_sem=self.send_sem.at[self.kind, phase * 2 + d],
            recv_sem=self.recv_sem.at[self.kind, first + self.slot(phase, d, t)],
            device_id=self.place.neighbour(axis, self.o(d)),
            device_id_type=MESH,
        )

    def send(self, phase, d, t, source):
        before = self.sent.pop((phase, d), None)
        if before is not None:
            before.wait_send()
        made = self.copy(phase, d, t, source)
        made.start()
        self.sent[(phase, d)] = made

    def dest(self, phase, d, t, count):
        axis = self.axes[phase]
        return wrap(self.place.pos[axis] + self.o(d) * (count - t + 1), self.place.size[axis])

    def begin(self, phase):
        for d, count in ring_dirs(self.place.size[self.axes[phase]]):
            self.send(phase, d, 1, self.term(phase, self.dest(phase, d, 1, count)))

    def advance(self, k):
        if k == 0:
            self.begin(0)
            return
        phase = 0 if k <= self.turns[0] else 1
        t = k - (self.turns[0] if phase else 0)
        axis = self.axes[phase]
        dirs = ring_dirs(self.place.size[axis])
        for d, count in dirs:
            if t <= count:
                held = self.arrived(phase, d, t)
                self.copy(phase, d, t, held).wait_recv()
                if t < count:
                    held[...] = held[...] + self.term(phase, self.dest(phase, d, t + 1, count))[...]
                    self.send(phase, d, t + 1, held)
        if t == self.turns[phase]:
            own = self.term(phase, self.place.pos[axis])
            total = own[...].astype(F32)
            for d, count in dirs:
                total = total + self.arrived(phase, d, count)[...].astype(F32)
            if phase == 0:
                own[...] = total.astype(BF16)
                self.begin(1)
            else:
                self.result = total

    def finish(self):
        for made in self.sent.values():
            made.wait_send()
        self.sent = {}


class RankSum:
    def __init__(self, place, parts, arrived, whole, sems):
        self.place, self.parts, self.got, self.whole, self.sems = place, parts, arrived, whole, sems

    def scatter_copy(self, j):
        peer = self.place.peer(j)
        return pltpu.make_async_remote_copy(
            src_ref=self.parts.at[peer[1]],
            dst_ref=self.got.at[j],
            send_sem=self.sems.at[0, j],
            recv_sem=self.sems.at[1, j],
            device_id=peer,
            device_id_type=MESH,
        )

    def gather_copy(self, j, at):
        return pltpu.make_async_remote_copy(
            src_ref=self.whole.at[at],
            dst_ref=self.whole.at[at],
            send_sem=self.sems.at[2, j],
            recv_sem=self.sems.at[3, j],
            device_id=self.place.peer(j),
            device_id_type=MESH,
        )

    def each(self, body):
        @pl.loop(1, self.place.nh)
        def _(j):
            body(j)

    def start(self):
        self.each(lambda j: self.scatter_copy(j).start())

    def middle(self):
        self.each(lambda j: self.scatter_copy(j).wait_recv())
        me = self.place.hid
        total = self.parts[me].astype(F32)
        for j in range(1, self.place.nh):
            total = total + self.got[j].astype(F32)
        self.whole[me] = total.astype(BF16)
        self.each(lambda j: self.gather_copy(j, me).start())

    def end(self):
        nh = self.place.nh

        def wait(j):
            self.gather_copy(j, lax.rem(self.place.hid + nh - j, nh)).wait_recv()

        self.each(wait)

    def finish(self):
        def wait(j):
            self.scatter_copy(j).wait_send()
            self.gather_copy(j, self.place.hid).wait_send()

        self.each(wait)


def layer(
    nx, nz, nh, scale,
    x_ref, g_ref, home, bu_ref, bd_ref, ul_ref, ur_ref, dl_ref, dr_ref,
    out_ref, ig_ref, gbu_ref, gbd_ref, gul_ref, gur_ref, gdl_ref, gdr_ref,
    g_low, g_up, g_down, t_low, t_up, t_down,
    low_z1, low_x2, low_x1, low_z2, up_z1, up_x2, up_x1, up_z2, dn_z1, dn_x2, dn_x1, dn_z2,
    w_up, w_down, m_low, xs, gs, xt, pre, der, hid_t, gp, hid_m, gp_m,
    rank_parts, rank_got, rank_one, rank_two,
    side_send, side_mid, side_end,
    ag_send, ag_recv, rs_send, rs_recv, rank_sems, y_sems,
):
    place = Place(nx, nz, nh)
    rows, blk = bu_ref.shape[2], bu_ref.shape[3]
    tokens = x_ref.shape[0]
    hb = bu_ref.shape[0]
    half = rows // 2
    px, pz = place.pos["x"], place.pos["z"]

    barrier = pltpu.get_barrier_semaphore()
    for axis in ("x", "z"):
        for o in (1, -1):
            pl.semaphore_signal(barrier, inc=1, device_id=place.neighbour(axis, o), device_id_type=MESH)

    @pl.loop(1, nh)
    def _(j):
        pl.semaphore_signal(barrier, inc=1, device_id=place.peer(j), device_id_type=MESH)

    hidden_dev, width_dev = ur_ref.shape[1], dr_ref.shape[1]
    g_low[px, pz, :, 0:hidden_dev] = jnp.concatenate(
        [ur_ref[...].astype(F32), dl_ref[...].astype(F32)], axis=0
    ).astype(BF16)
    g_low[px, pz, :, hidden_dev:] = jnp.concatenate(
        [ul_ref[...].astype(F32), dr_ref[...].astype(F32)], axis=0
    ).astype(BF16)
    for s in range(SLOTS):
        for h in range(hb):
            at = (s * hb + h) * blk
            g_up[px, pz, :, at : at + blk] = bu_ref[h, s]
            g_down[px, pz, :, at : at + blk] = bd_ref[h, s]
    for b in range(2):
        xs[0, b] = x_ref[:, b * blk : (b + 1) * blk]
        gs[0, b] = g_ref[:, b * blk : (b + 1) * blk]
    pl.semaphore_wait(barrier, 4 + nh - 1)

    groups = (g_low, g_up, g_down)
    gathers = [
        [
            Gather(place, buf, kind, buf.shape[3] // 4, ag_send.at[i], ag_recv.at[i])
            for kind in range(4)
        ]
        for i, buf in enumerate(groups)
    ]
    rounds = nx // 2 + nz // 2

    def gather_step(i, k):
        for one in gathers[i]:
            one.advance(k)

    part = tokens // 2
    pieces = [(ref, b, q) for ref in (xs, gs) for b in range(2) for q in range(2)]

    def y_copy(i, stage):
        ref, b, q = pieces[i]
        at = pl.ds(q * part, part)
        return pltpu.make_async_remote_copy(
            src_ref=ref.at[0 if stage == 0 else 2, b, at],
            dst_ref=ref.at[2 if stage == 0 else 1, b, at],
            send_sem=y_sems.at[stage, 0, i],
            recv_sem=y_sems.at[stage, 1, i],
            device_id=place.near if stage == 0 else place.far,
            device_id_type=MESH,
        )

    gather_step(0, 0)
    for i in range(4):
        y_copy(i, 0).start()
    gather_step(1, 0)
    for i in range(4, 8):
        y_copy(i, 0).start()
    gather_step(2, 0)

    def pass_on(i):
        y_copy(i, 0).wait_recv()
        y_copy(i, 1).start()

    column = lax.broadcasted_iota(jnp.int32, (tokens, blk), 1)
    is_low = lax.rem(column, rows) < half

    def flat(buf, at, width):
        return buf[:, :, :, at : at + width].astype(F32).reshape(blk, width).astype(BF16)

    one = RankSum(place, rank_parts.at[0], rank_got.at[0], rank_one, rank_sems.at[0])
    two = RankSum(place, rank_parts.at[1], rank_got.at[1], rank_two, rank_sems.at[1])

    def rank_start(which, index, low, high):
        mixed = jnp.where(is_low, low, high).reshape(nh, tokens // nh, blk)
        rank_parts[index] = mixed.astype(BF16)
        which.start()

    passed = 0
    for k in range(1, rounds + 3):
        for i in range(3):
            if 1 <= k - i <= rounds:
                gather_step(i, k - i)
        if k == rounds:
            for j in range(6):
                m_low[:, j * blk : (j + 1) * blk] = flat(g_low, j * blk, blk)
            rank_start(
                one,
                0,
                dot(x_ref[...], m_low[:, hidden_dev:], NT),
                dot(g_ref[...], m_low[:, hidden_dev:], NT),
            )
        while passed < min(8, k):
            pass_on(passed)
            passed += 1
        if k == rounds + 1:
            for j in range(SLOTS * hb):
                w_up[j // hb, :, (j % hb) * blk : (j % hb + 1) * blk] = flat(g_up, j * blk, blk)
    while passed < 8:
        pass_on(passed)
        passed += 1
    one.middle()
    for j in range(SLOTS * hb):
        w_down[j // hb, (j % hb) * blk : (j % hb + 1) * blk, :] = flat(g_down, j * blk, blk)
    for i in range(8):
        y_copy(i, 1).wait_recv()
    for s in range(SLOTS):
        for b in range(2):
            xt[s, b] = xs[s, b].T

    one.end()
    rank1 = rank_one[...].reshape(tokens, blk)
    zero = jnp.zeros_like(rank1)
    rank_in = jnp.where(is_low, rank1, zero)
    rank_back = jnp.where(is_low, zero, rank1)

    @pl.loop(0, hb)
    def _(h):
        home_h = home[h]
        at = pl.ds(pl.multiple_of(h * blk, blk), blk)
        value = dot(rank_in, m_low[:, at])
        grad = dot(rank_back, m_low[:, at])
        for s in range(SLOTS):
            value = value + dot(xs[s, home_h], w_up[s, :, at])
            grad = grad + dot(gs[s, home_h], w_down[s, at, :], NT)
        activated, derivative = gelu_pair(value)
        hidden = activated.astype(BF16)
        grad_pre = (grad * derivative).astype(BF16)
        hid_t[h] = hidden.T
        gp[h] = grad_pre
        for b in range(2):
            keep = jnp.where(home_h == b, 1.0, 0.0).astype(F32)
            hid_m[b, :, at] = (hidden.astype(F32) * keep).astype(BF16)
            gp_m[b, :, at] = (grad_pre.astype(F32) * keep).astype(BF16)

    def side(tensor, s, b):
        if tensor == 0:
            return dot(hid_m[b], w_down[s])
        return dot(gp_m[b], w_up[s], NT)

    sides = [(tensor, b) for tensor in range(2) for b in range(2)]

    def side_copy(i, stage):
        tensor, b = sides[i]
        return pltpu.make_async_remote_copy(
            src_ref=(side_send if stage == 0 else side_mid).at[tensor, b],
            dst_ref=(side_mid if stage == 0 else side_end).at[tensor, b],
            send_sem=y_sems.at[2 + stage, 0, i],
            recv_sem=y_sems.at[2 + stage, 1, i],
            device_id=place.far if stage == 0 else place.near,
            device_id_type=MESH,
        )

    for i, (tensor, b) in enumerate(sides):
        side_send[tensor, b] = side(tensor, 1, b).astype(BF16)
        side_copy(i, 0).start()

    hidden_all = hid_m[0] + hid_m[1]
    grad_all = gp_m[0] + gp_m[1]
    rank_start(
        two, 1, dot(grad_all, m_low[:, 0:hidden_dev], NT), dot(hidden_all, m_low[:, 0:hidden_dev], NT)
    )

    bufs = (
        (low_z1, low_x2, low_x1, low_z2),
        (up_z1, up_x2, up_x1, up_z2),
        (dn_z1, dn_x2, dn_x1, dn_z2),
    )
    terms = (t_low, t_up, t_down)
    scatters = [
        [
            Scatter(
                place, terms[i], kind, terms[i].shape[3] // 4,
                *(bufs[i][0:2] if kind < 2 else bufs[i][2:4]),
                rs_send.at[i], rs_recv.at[i],
            )
            for kind in range(4)
        ]
        for i in range(3)
    ]

    def scatter_step(i, k):
        for one_chunk in scatters[i]:
            one_chunk.advance(k)

    def shaped(value):
        return (value * scale).reshape(nx, nz, rows, value.shape[1]).astype(BF16)

    @pl.loop(0, hb)
    def _(h):
        home_h = home[h]
        for s in range(SLOTS):
            at = pl.ds(pl.multiple_of((s * hb + h) * blk, blk), blk)
            t_up[:, :, :, at] = shaped(dot(xt[s, home_h], gp[h]))

    scatter_step(1, 0)

    @pl.loop(0, hb)
    def _(h):
        home_h = home[h]
        for s in range(SLOTS):
            at = pl.ds(pl.multiple_of((s * hb + h) * blk, blk), blk)
            t_down[:, :, :, at] = shaped(dot(hid_t[h], gs[s, home_h]))

    scatter_step(2, 0)

    def side_pass(i):
        tensor, b = sides[i]
        own = side(tensor, 2, b)
        side_copy(i, 0).wait_recv()
        side_mid[tensor, b] = (side_mid[tensor, b].astype(F32) + own).astype(BF16)
        side_copy(i, 1).start()

    rank_in_t = rank_in.T
    rank_back_t = rank_back.T
    for j in range(hb):
        at = slice(j * blk, (j + 1) * blk)
        t_low[:, :, :, at] = shaped(
            dot(rank_in_t, grad_all[:, at]) + dot(rank_back_t, hidden_all[:, at])
        )
    scatter_step(1, 1)
    two.middle()
    side_pass(0)
    scatter_step(2, 1)
    scatter_step(1, 2)
    side_pass(1)
    two.end()
    rank2 = rank_two[...].reshape(tokens, blk)
    rank_grad = jnp.where(is_low, rank2, zero)
    rank_mid = jnp.where(is_low, zero, rank2)
    rank_grad_t = rank_grad.T
    rank_mid_t = rank_mid.T
    for j in range(2):
        at = slice(j * blk, (j + 1) * blk)
        to = slice(hidden_dev + j * blk, hidden_dev + (j + 1) * blk)
        t_low[:, :, :, to] = shaped(
            dot(rank_grad_t, x_ref[:, at]) + dot(rank_mid_t, g_ref[:, at])
        )
    scatter_step(0, 0)
    scatter_step(2, 2)
    scatter_step(1, 3)
    scatter_step(0, 1)
    side_pass(2)
    for k in range(3, rounds + 1):
        scatter_step(2, k)
        if k + 1 <= rounds:
            scatter_step(1, k + 1)
        scatter_step(0, k - 1)
        if k == 3:
            side_pass(3)
    scatter_step(0, rounds)

    for i, (tensor, b) in enumerate(sides):
        at = slice(b * blk, (b + 1) * blk)
        to = slice(hidden_dev + b * blk, hidden_dev + (b + 1) * blk)
        rank = rank_mid if tensor == 0 else rank_grad
        total = side(tensor, 0, b) + dot(rank, m_low[:, to])
        side_copy(i, 1).wait_recv()
        total = total + side_end[tensor, b].astype(F32)
        ref = out_ref if tensor == 0 else ig_ref
        ref[:, at] = total.astype(BF16)

    def whole(i):
        return jnp.concatenate([one_chunk.result for one_chunk in scatters[i]], axis=1)

    for i, ref in ((1, gbu_ref), (2, gbd_ref)):
        total = whole(i).astype(BF16)
        for s in range(SLOTS):
            for h in range(hb):
                at = (s * hb + h) * blk
                ref[h, s] = total[:, at : at + blk]
    low = whole(0)
    gur_ref[...] = low[:half, :hidden_dev].astype(BF16)
    gdl_ref[...] = low[half:, :hidden_dev].astype(BF16)
    gul_ref[...] = low[:half, hidden_dev:].astype(BF16)
    gdr_ref[...] = low[half:, hidden_dev:].astype(BF16)

    for i in range(3):
        for kind in range(4):
            gathers[i][kind].finish()
            scatters[i][kind].finish()
    for i in range(8):
        y_copy(i, 0).wait_send()
        y_copy(i, 1).wait_send()
    for i in range(4):
        side_copy(i, 0).wait_send()
        side_copy(i, 1).wait_send()
    one.finish()
    two.finish()


def per_device(
    nx, nz, nh,
    inputs, out_grad, home_block, blocks_up, blocks_down, up_left, up_right, down_left, down_right,
):
    tokens, width_dev = inputs.shape
    hb, slots, rows, blk = blocks_up.shape
    hidden_dev = hb * blk
    scale = float(nx * nz * tokens) ** (-0.5)
    low_cols, blk_cols = hidden_dev + width_dev, slots * hb * blk
    vmem = pl.BlockSpec(memory_space=pltpu.VMEM)
    smem = pl.BlockSpec(memory_space=pltpu.SMEM)

    def buf(shape, dtype=BF16):
        return pltpu.VMEM(shape, dtype)

    gathered = [buf((nx, nz, rows, c)) for c in (low_cols, blk_cols, blk_cols)]
    landing = []
    for c in (low_cols, blk_cols, blk_cols):
        w = c // 4
        landing += [
            buf((2, nz - 1, nx, rows, w)),
            buf((2, nx - 1, rows, w)),
            buf((2, nx - 1, nz, rows, w)),
            buf((2, nz - 1, rows, w)),
        ]
    ups = up_left.T, down_left.T
    outs = pl.pallas_call(
        functools.partial(layer, nx, nz, nh, scale),
        out_shape=[
            jax.ShapeDtypeStruct(a.shape, BF16)
            for a in (
                inputs, out_grad, blocks_up, blocks_down, ups[0], up_right, ups[1], down_right,
            )
        ],
        in_specs=[vmem, vmem, smem] + [vmem] * 6,
        out_specs=[vmem] * 8,
        scratch_shapes=gathered
        + gathered
        + landing
        + [
            buf((slots, blk, hidden_dev)),
            buf((slots, hidden_dev, blk)),
            buf((blk, low_cols)),
            buf((slots, 2, tokens, blk)),
            buf((slots, 2, tokens, blk)),
            buf((slots, 2, blk, tokens)),
            buf((8, 128), F32),
            buf((8, 128), F32),
            buf((hb, blk, tokens)),
            buf((hb, tokens, blk)),
            buf((2, tokens, hidden_dev)),
            buf((2, tokens, hidden_dev)),
            buf((2, nh, tokens // nh, blk)),
            buf((2, nh, tokens // nh, blk)),
            buf((nh, tokens // nh, blk)),
            buf((nh, tokens // nh, blk)),
            buf((2, 2, tokens, blk)),
            buf((2, 2, tokens, blk)),
            buf((2, 2, tokens, blk)),
            pltpu.SemaphoreType.DMA((3, 4, 4)),
            pltpu.SemaphoreType.DMA((3, 4, nx + nz - 2)),
            pltpu.SemaphoreType.DMA((3, 4, 4)),
            pltpu.SemaphoreType.DMA((3, 4, nx + nz - 2)),
            pltpu.SemaphoreType.DMA((2, 4, nh)),
            pltpu.SemaphoreType.DMA((4, 2, 8)),
        ],
        compiler_params=pltpu.CompilerParams(
            collective_id=0, has_side_effects=True, vmem_limit_bytes=60 * 2**20
        ),
    )(
        inputs, out_grad, home_block, blocks_up, blocks_down, ups[0], up_right, ups[1], down_right,
    )
    out, ig, gbu, gbd, gul, gur, gdl, gdr = outs
    return out, ig, gbu, gbd, gul.T, gur, gdl.T, gdr


def solution(mesh, nx=4):
    n_dp, nh = mesh.shape["dp"], mesh.shape["hid"]
    placed = (
        P("dp", "hid"),
        P("dp", "hid"),
        P("hid"),
        P("hid", None, "dp", None),
        P("hid", None, "dp", None),
        P("hid", "dp"),
        P("dp", "hid"),
        P("hid", "dp"),
        P("dp", "hid"),
    )
    return jax.shard_map(
        functools.partial(per_device, nx, n_dp // nx, nh),
        mesh=mesh,
        in_specs=placed,
        out_specs=(
            P("dp", "hid"),
            P("dp", "hid"),
            P("hid", None, "dp", None),
            P("hid", None, "dp", None),
            P("hid", "dp"),
            P("dp", "hid"),
            P("hid", "dp"),
            P("dp", "hid"),
        ),
        check_vma=False,
    )
```

time: 740 us -> 148 us (0.20)
  waiting for transfers between devices: 342 us -> 0 us
  blocking collectives: 281 us -> 0 us
  Pallas kernels: 0 us -> 138 us
  starting transfers between devices: 33 us -> 0 us
  local copies, waits for them, and re-layouts: 33.8 us -> 6.67 us
  matrix products: 25.2 us -> 0 us
  between operations: 15.5 us -> 0.66 us
    unnamed x6 -> x0, waiting for transfers between devices: 266 us -> none
    all_gather x4 -> x0, blocking collectives: 148 us -> none  [the longest x1 41.8 us: per_device(): lax.all_gather(up_left, 'dp', axis=1, tiled=True)]
    pallas_call x0 -> x1, Pallas kernels: none -> 138 us  [per_device(): pl.pallas_call(functools.partial(layer, nx, nz, nh, scale), out_shape=[ja...]
    psum x2 -> x0, blocking collectives: 133 us -> none  [the longest x1 73.3 us: per_device(): lax.psum(jnp.dot(inputs, left_in, preferred_element_type=single), 'hid')]
    ppermute x8 -> x0, waiting for transfers between devices: 76 us -> none  [from_partner(): return lax.ppermute(value, axis, pairs)]
    ppermute x8 -> x0, starting transfers between devices: 32.7 us -> none  [from_partner(): return lax.ppermute(value, axis, pairs)]
    dot_general x20 -> x0, matrix products: 25.2 us -> none  [the longest x1 4.08 us: per_device(): placed = jnp.einsum('sthn,hi->stin', down_sum, select, precision=highest)]
    unnamed x49 -> x22, local copies, waits for them, and re-layouts: 19.2 us -> 6.67 us
  transfers between devices with their start and end apart: 12 -> 0, of which waited for: 5 -> 0; matrix products, arithmetic and copies ran while one was open for 6% -> 0% of each run, Pallas kernels for 0% -> 0%
where the time goes in v1:
time: 148 us; the launch traced here: 145 us
  Pallas kernels  138 us (93%)
  local copies, waits for them, and re-layouts  6.67 us (5%)
    pallas_call x1, Pallas kernels, per_device(): pl.pallas_call(functools.partial(layer, nx, nz, nh, scale), out_shape=[ja...  138 us
    unnamed x22, local copies, waits for them, and re-layouts  6.67 us

profile of v1, /device:TPU:1, one launch (start us, length us, event | category | flops | bytes accessed | tf_op | source)
XLA Modules:
  0.0 145.5 jit_solution(8191813400809669949)
XLA Ops:
  0.6 138.2 %shard_map.152 = (bf16[256,512]{1,0:T(8,128)(2,1)}, bf16[256,512]{1,0:T(8,128)(2,1)}, bf16[4,3,8,256]{3,2,1,0:T(8,128)(2,1)}, bf16[4,3,8,256]{3,2,1,0:T(8,128)(2...) custom-call(bf16[256,512]{1,0:T(8,128)(2,1)} %x_ref.1, ...), custom_call_target="tpu_custom_call" | custom-call | tf_op jit(solution)/shard_map/pallas_call | solution.py:626
  138.8 0.0 copy-start
  138.8 1.7 %copy.25 = bf16[256,512]{1,0:T(8,128)(2,1)} copy(bf16[256,512]{1,0:T(8,128)(2,1)} %get-tuple-element.32) | data formatting | bytes 524288
  140.5 0.0 copy-done
  140.5 0.0 copy-start.2
  140.5 0.7 copy.26
  141.2 0.1 copy-done.2
  141.3 0.0 copy-start.1
  141.3 0.6 copy.27
  141.9 0.2 copy-done.1
  142.1 0.0 copy-start.6
  142.1 0.6 copy.28
  142.8 0.1 copy-done.6
  142.8 0.0 copy-start.4
  142.8 0.6 copy.29
  143.4 0.1 copy-done.4
  143.5 0.0 copy-start.3
  143.5 0.6 copy.30
  144.1 0.1 copy-done.3
  144.2 0.0 copy-start.5
  144.2 0.6 copy.31
  144.8 0.1 copy-done.5
  144.9 0.6 copy.32
Async XLA Ops:
  138.8 1.7 %copy-start = (bf16[256,512]{1,0:T(8,128)(2,1)S(1)}, bf16[256,512]{1,0:T(8,128)(2,1)}, u32[]{:S(2)}) copy-start(bf16[256,512]{1,0:T(8,128)(2,1)} %get-tuple-element.33) | copy-start | bytes 786436
  140.5 0.8 copy-start.2
  141.3 0.8 copy-start.1
  142.1 0.7 copy-start.6
  142.8 0.7 copy-start.4
  143.5 0.7 copy-start.3
  144.2 0.7 copy-start.5

commit v2 on v1

--- a/solution.py
+++ b/solution.py
@@ -68,72 +68,86 @@
     return [(0, n // 2)] + ([(1, n // 2 - 1)] if n > 2 else [])
 
 
-class Gather:
-    def __init__(self, place, buf, kind, width, send_sem, recv_sem):
+class TorusGather:
+    def __init__(self, place, buf, kind, send_sem, recv_sem):
         self.place, self.buf, self.kind = place, buf, kind
-        self.columns = pl.ds(kind * width, width)
+        self.width = buf.shape[3] // 2
+        self.axes = ("x", "z") if kind == 0 else ("z", "x")
+        self.n = [place.size[a] for a in self.axes]
         self.send_sem, self.recv_sem = send_sem, recv_sem
-        self.axes = gather_axes(kind)
-        self.turns = [place.size[a] // 2 for a in self.axes]
-        self.rounds = sum(self.turns)
-        self.sent = {}
-
-    def part(self, phase, at):
-        axis = self.axes[phase]
-        own = self.place.pos
-        if phase == 0:
-            x, z = (at, own["z"]) if axis == "x" else (own["x"], at)
-            return self.buf.at[x, z, :, self.columns]
-        if axis == "x":
-            return self.buf.at[at, :, :, self.columns]
-        return self.buf.at[:, at, :, self.columns]
-
-    def copy(self, phase, d, t, at):
-        axis = self.axes[phase]
-        o = (1 if self.kind % 2 == 0 else -1) * (1 if d == 0 else -1)
-        n = self.place.size[axis]
-        first = 0 if phase == 0 else self.place.size[self.axes[0]] - 1
-        slot = first + (n // 2 if d else 0) + t - 1
-        ref = self.part(phase, wrap(self.place.pos[axis] - o * at, n))
+        self.rounds = self.n[0] // 2 + self.n[1] // 2
+        self.sent = []
+        self.count = 0
+        self.ids = {}
+
+    def view(self, f, g, part):
+        at = {}
+        for axis, n, off in zip(self.axes, self.n, (f, g)):
+            at[axis] = wrap(self.place.pos[axis] - off, n)
+        first = self.kind * self.width
+        width = self.width
+        if part is not None:
+            width = width // 2
+            first = first + part * width
+        return self.buf.at[at["x"], at["z"], :, pl.ds(first, width)]
+
+    def copy(self, level, f, g, o, ref):
+        at = self.ids.setdefault((level, f, g, o), len(self.ids))
         return pltpu.make_async_remote_copy(
             src_ref=ref,
             dst_ref=ref,
-            send_sem=self.send_sem.at[self.kind, phase * 2 + d],
-            recv_sem=self.recv_sem.at[self.kind, slot],
-            device_id=self.place.neighbour(axis, o),
+            send_sem=self.send_sem.at[self.kind, at],
+            recv_sem=self.recv_sem.at[self.kind, at],
+            device_id=self.place.neighbour(self.axes[level], o),
             device_id_type=MESH,
         )
 
-    def send(self, phase, d, t):
-        before = self.sent.pop((phase, d), None)
-        if before is not None:
-            before.wait_send()
-        made = self.copy(phase, d, t, t - 1)
+    def send(self, level, f, g, o, part):
+        made = self.copy(level, f, g, o, self.view(f, g, part))
         made.start()
-        self.sent[(phase, d)] = made
-
-    def begin(self, phase):
-        for d, count in ring_dirs(self.place.size[self.axes[phase]]):
-            self.send(phase, d, 1)
+        self.sent.append(made)
+
+    def spread(self, level, f, g):
+        here = f if level == 0 else g
+        half = self.n[level] // 2
+        for o in (1, -1):
+            if here * o < 0 or abs(here) >= half:
+                continue
+            part = None if abs(here) + 1 < half else (0 if o > 0 else 1)
+            self.send(level, f, g, o, part)
+
+    def stops(self, level):
+        half = self.n[level] // 2
+        return [(0, 0)] + [(o * t, t) for t in range(1, half) for o in (1, -1)] + [(half, half)]
+
+    def arrive(self, level, f, g):
+        here = f if level == 0 else g
+        half = self.n[level] // 2
+        for o in (1, -1):
+            if here * o < 0 and abs(here) < half:
+                continue
+            last = o * (abs(here) - 1)
+            back = (last, g) if level == 0 else (f, last)
+            part = None if abs(here) < half else (0 if o > 0 else 1)
+            self.copy(level, *back, o, self.view(f, g, part)).wait_recv()
 
     def advance(self, k):
-        if k == 0:
-            self.begin(0)
-            return
-        phase = 0 if k <= self.turns[0] else 1
-        t = k - (self.turns[0] if phase else 0)
-        for d, count in ring_dirs(self.place.size[self.axes[phase]]):
-            if t <= count:
-                self.copy(phase, d, t, t).wait_recv()
-                if t < count:
-                    self.send(phase, d, t + 1)
-        if phase == 0 and t == self.turns[0]:
-            self.begin(1)
+        for f, a in self.stops(0):
+            if a == k:
+                if a:
+                    self.arrive(0, f, 0)
+                self.spread(0, f, 0)
+                self.spread(1, f, 0)
+        for f, a in self.stops(0):
+            for g, b in self.stops(1):
+                if b and a + b == k:
+                    self.arrive(1, f, g)
+                    self.spread(1, f, g)
 
     def finish(self):
-        for made in self.sent.values():
+        for made in self.sent:
             made.wait_send()
-        self.sent = {}
+        self.sent = []
 
 
 class Scatter:
@@ -227,6 +241,97 @@
         self.sent = {}
 
 
+class DirectGather:
+    def __init__(self, place, buf, sems):
+        self.place, self.buf, self.sems = place, buf, sems
+
+    def copies(self, phase, sending):
+        place = self.place
+        axis = "xz"[phase]
+        n = place.size[axis]
+        made = []
+        for j in range(1, n):
+            if phase == 0:
+                at = place.pos["x"] if sending else wrap(place.pos["x"] - j, n)
+                ref = self.buf.at[at, place.pos["z"]]
+            else:
+                at = place.pos["z"] if sending else wrap(place.pos["z"] - j, n)
+                ref = self.buf.at[:, at]
+            made.append(
+                pltpu.make_async_remote_copy(
+                    src_ref=ref,
+                    dst_ref=ref,
+                    send_sem=self.sems.at[0, phase, j],
+                    recv_sem=self.sems.at[1, phase, j],
+                    device_id=place.neighbour(axis, j),
+                    device_id_type=MESH,
+                )
+            )
+        return made
+
+    def begin(self, phase):
+        for made in self.copies(phase, True):
+            made.start()
+
+    def wait(self, phase):
+        for made in self.copies(phase, False):
+            made.wait_recv()
+
+    def finish(self):
+        for phase in range(2):
+            for made in self.copies(phase, True):
+                made.wait_send()
+
+
+class DirectScatter:
+    def __init__(self, place, terms, first_buf, second_buf, sems):
+        self.place, self.terms, self.sems = place, terms, sems
+        self.bufs = (first_buf, second_buf)
+
+    def term(self, phase, at):
+        if phase == 0:
+            return self.terms.at[:, at]
+        return self.terms.at[at, self.place.pos["z"]]
+
+    def copies(self, phase):
+        place = self.place
+        axis = "zx"[phase]
+        n = place.size[axis]
+        return [
+            pltpu.make_async_remote_copy(
+                src_ref=self.term(phase, wrap(place.pos[axis] + j, n)),
+                dst_ref=self.bufs[phase].at[j],
+                send_sem=self.sems.at[0, phase, j],
+                recv_sem=self.sems.at[1, phase, j],
+                device_id=place.neighbour(axis, j),
+                device_id_type=MESH,
+            )
+            for j in range(1, n)
+        ]
+
+    def begin(self, phase):
+        for made in self.copies(phase):
+            made.start()
+
+    def wait(self, phase):
+        axis = "zx"[phase]
+        for made in self.copies(phase):
+            made.wait_recv()
+        own = self.term(phase, self.place.pos[axis])
+        total = own[...].astype(F32)
+        for j in range(1, self.place.size[axis]):
+            total = total + self.bufs[phase][j].astype(F32)
+        if phase == 0:
+            own[...] = total.astype(BF16)
+        else:
+            self.result = total
+
+    def finish(self):
+        for phase in range(2):
+            for made in self.copies(phase):
+                made.wait_send()
+
+
 class RankSum:
     def __init__(self, place, parts, arrived, whole, sems):
         self.place, self.parts, self.got, self.whole, self.sems = place, parts, arrived, whole, sems
@@ -289,12 +394,12 @@
     nx, nz, nh, scale,
     x_ref, g_ref, home, bu_ref, bd_ref, ul_ref, ur_ref, dl_ref, dr_ref,
     out_ref, ig_ref, gbu_ref, gbd_ref, gul_ref, gur_ref, gdl_ref, gdr_ref,
-    g_low, g_up, g_down, t_low, t_up, t_down,
-    low_z1, low_x2, low_x1, low_z2, up_z1, up_x2, up_x1, up_z2, dn_z1, dn_x2, dn_x1, dn_z2,
-    w_up, w_down, m_low, xs, gs, xt, pre, der, hid_t, gp, hid_m, gp_m,
+    g_low, g_all, t_low, t_all,
+    low_first, low_second, all_z1, all_x2, all_x1, all_z2,
+    w_up, w_down, m_one, m_two, xs, gs, xt, hid_t, gp, hid_m, gp_m,
     rank_parts, rank_got, rank_one, rank_two,
     side_send, side_mid, side_end,
-    ag_send, ag_recv, rs_send, rs_recv, rank_sems, y_sems,
+    ag_send, ag_recv, rs_send, rs_recv, rank_sems, low_sems, y_sems,
 ):
     place = Place(nx, nz, nh)
     rows, blk = bu_ref.shape[2], bu_ref.shape[3]
@@ -305,7 +410,7 @@
 
     barrier = pltpu.get_barrier_semaphore()
     for axis in ("x", "z"):
-        for o in (1, -1):
+        for o in range(1, place.size[axis]):
             pl.semaphore_signal(barrier, inc=1, device_id=place.neighbour(axis, o), device_id_type=MESH)
 
     @pl.loop(1, nh)
@@ -313,35 +418,29 @@
         pl.semaphore_signal(barrier, inc=1, device_id=place.peer(j), device_id_type=MESH)
 
     hidden_dev, width_dev = ur_ref.shape[1], dr_ref.shape[1]
-    g_low[px, pz, :, 0:hidden_dev] = jnp.concatenate(
+    g_low[px, pz] = jnp.concatenate([ul_ref[...].astype(F32), dr_ref[...].astype(F32)], axis=0).astype(BF16)
+    downs = SLOTS * hb * blk
+    ranks = 2 * downs
+    g_all[px, pz, :, ranks:] = jnp.concatenate(
         [ur_ref[...].astype(F32), dl_ref[...].astype(F32)], axis=0
-    ).astype(BF16)
-    g_low[px, pz, :, hidden_dev:] = jnp.concatenate(
-        [ul_ref[...].astype(F32), dr_ref[...].astype(F32)], axis=0
     ).astype(BF16)
     for s in range(SLOTS):
         for h in range(hb):
             at = (s * hb + h) * blk
-            g_up[px, pz, :, at : at + blk] = bu_ref[h, s]
-            g_down[px, pz, :, at : at + blk] = bd_ref[h, s]
+            g_all[px, pz, :, at : at + blk] = bu_ref[h, s]
+            g_all[px, pz, :, downs + at : downs + at + blk] = bd_ref[h, s]
     for b in range(2):
         xs[0, b] = x_ref[:, b * blk : (b + 1) * blk]
         gs[0, b] = g_ref[:, b * blk : (b + 1) * blk]
-    pl.semaphore_wait(barrier, 4 + nh - 1)
-
-    groups = (g_low, g_up, g_down)
-    gathers = [
-        [
-            Gather(place, buf, kind, buf.shape[3] // 4, ag_send.at[i], ag_recv.at[i])
-            for kind in range(4)
-        ]
-        for i, buf in enumerate(groups)
-    ]
+    pl.semaphore_wait(barrier, nx + nz + nh - 3)
+
+    gathers = [TorusGather(place, g_all, kind, ag_send, ag_recv) for kind in range(2)]
+    low_gather = DirectGather(place, g_low, low_sems.at[0])
     rounds = nx // 2 + nz // 2
 
-    def gather_step(i, k):
-        for one in gathers[i]:
-            one.advance(k)
+    def gather_step(k):
+        for one_half in gathers:
+            one_half.advance(k)
 
     part = tokens // 2
     pieces = [(ref, b, q) for ref in (xs, gs) for b in range(2) for q in range(2)]
@@ -358,14 +457,6 @@
             device_id_type=MESH,
         )
 
-    gather_step(0, 0)
-    for i in range(4):
-        y_copy(i, 0).start()
-    gather_step(1, 0)
-    for i in range(4, 8):
-        y_copy(i, 0).start()
-    gather_step(2, 0)
-
     def pass_on(i):
         y_copy(i, 0).wait_recv()
         y_copy(i, 1).start()
@@ -384,39 +475,48 @@
         rank_parts[index] = mixed.astype(BF16)
         which.start()
 
-    passed = 0
-    for k in range(1, rounds + 3):
-        for i in range(3):
-            if 1 <= k - i <= rounds:
-                gather_step(i, k - i)
-        if k == rounds:
-            for j in range(6):
-                m_low[:, j * blk : (j + 1) * blk] = flat(g_low, j * blk, blk)
-            rank_start(
-                one,
-                0,
-                dot(x_ref[...], m_low[:, hidden_dev:], NT),
-                dot(g_ref[...], m_low[:, hidden_dev:], NT),
-            )
-        while passed < min(8, k):
-            pass_on(passed)
-            passed += 1
-        if k == rounds + 1:
-            for j in range(SLOTS * hb):
-                w_up[j // hb, :, (j % hb) * blk : (j % hb + 1) * blk] = flat(g_up, j * blk, blk)
-    while passed < 8:
-        pass_on(passed)
-        passed += 1
+    low_gather.begin(0)
+    gather_step(0)
+    for i in range(4):
+        y_copy(i, 0).start()
+    low_gather.wait(0)
+    low_gather.begin(1)
+    gather_step(1)
+    for i in range(4, 8):
+        y_copy(i, 0).start()
+    pass_on(0)
+    gather_step(2)
+    low_gather.wait(1)
+    for j in range(2):
+        m_two[:, j * blk : (j + 1) * blk] = flat(g_low, j * blk, blk)
+    rank_start(one, 0, dot(x_ref[...], m_two[...], NT), dot(g_ref[...], m_two[...], NT))
+    pass_on(1)
+    pass_on(2)
+    gather_step(3)
+    pass_on(3)
+    pass_on(4)
+    gather_step(4)
     one.middle()
-    for j in range(SLOTS * hb):
-        w_down[j // hb, (j % hb) * blk : (j % hb + 1) * blk, :] = flat(g_down, j * blk, blk)
-    for i in range(8):
+    pass_on(5)
+    gather_step(5)
+    pass_on(6)
+    pass_on(7)
+    for i in range(4):
         y_copy(i, 1).wait_recv()
     for s in range(SLOTS):
         for b in range(2):
             xt[s, b] = xs[s, b].T
-
     one.end()
+    for k in range(6, rounds + 1):
+        gather_step(k)
+    for j in range(SLOTS * hb):
+        w_up[j // hb, :, (j % hb) * blk : (j % hb + 1) * blk] = flat(g_all, j * blk, blk)
+        w_down[j // hb, (j % hb) * blk : (j % hb + 1) * blk, :] = flat(g_all, downs + j * blk, blk)
+    for j in range(hb):
+        m_one[:, j * blk : (j + 1) * blk] = flat(g_all, ranks + j * blk, blk)
+    for i in range(4, 8):
+        y_copy(i, 1).wait_recv()
+
     rank1 = rank_one[...].reshape(tokens, blk)
     zero = jnp.zeros_like(rank1)
     rank_in = jnp.where(is_low, rank1, zero)
@@ -426,8 +526,8 @@
     def _(h):
         home_h = home[h]
         at = pl.ds(pl.multiple_of(h * blk, blk), blk)
-        value = dot(rank_in, m_low[:, at])
-        grad = dot(rank_back, m_low[:, at])
+        value = dot(rank_in, m_one[:, at])
+        grad = dot(rank_back, m_one[:, at])
         for s in range(SLOTS):
             value = value + dot(xs[s, home_h], w_up[s, :, at])
             grad = grad + dot(gs[s, home_h], w_down[s, at, :], NT)
@@ -459,36 +559,27 @@
             device_id_type=MESH,
         )
 
+    hidden_all = hid_m[0] + hid_m[1]
+    grad_all = gp_m[0] + gp_m[1]
+    rank_start(
+        two, 1, dot(grad_all, m_one[...], NT), dot(hidden_all, m_one[...], NT)
+    )
     for i, (tensor, b) in enumerate(sides):
         side_send[tensor, b] = side(tensor, 1, b).astype(BF16)
         side_copy(i, 0).start()
 
-    hidden_all = hid_m[0] + hid_m[1]
-    grad_all = gp_m[0] + gp_m[1]
-    rank_start(
-        two, 1, dot(grad_all, m_low[:, 0:hidden_dev], NT), dot(hidden_all, m_low[:, 0:hidden_dev], NT)
-    )
-
-    bufs = (
-        (low_z1, low_x2, low_x1, low_z2),
-        (up_z1, up_x2, up_x1, up_z2),
-        (dn_z1, dn_x2, dn_x1, dn_z2),
-    )
-    terms = (t_low, t_up, t_down)
     scatters = [
-        [
-            Scatter(
-                place, terms[i], kind, terms[i].shape[3] // 4,
-                *(bufs[i][0:2] if kind < 2 else bufs[i][2:4]),
-                rs_send.at[i], rs_recv.at[i],
-            )
-            for kind in range(4)
-        ]
-        for i in range(3)
+        Scatter(
+            place, t_all, kind, t_all.shape[3] // 4,
+            *((all_z1, all_x2) if kind < 2 else (all_x1, all_z2)),
+            rs_send, rs_recv,
+        )
+        for kind in range(4)
     ]
-
-    def scatter_step(i, k):
-        for one_chunk in scatters[i]:
+    low_scatter = DirectScatter(place, t_low, low_first, low_second, low_sems.at[1])
+
+    def scatter_step(k):
+        for one_chunk in scatters:
             one_chunk.advance(k)
 
     def shaped(value):
@@ -499,18 +590,18 @@
         home_h = home[h]
         for s in range(SLOTS):
             at = pl.ds(pl.multiple_of((s * hb + h) * blk, blk), blk)
-            t_up[:, :, :, at] = shaped(dot(xt[s, home_h], gp[h]))
-
-    scatter_step(1, 0)
-
-    @pl.loop(0, hb)
-    def _(h):
-        home_h = home[h]
-        for s in range(SLOTS):
-            at = pl.ds(pl.multiple_of((s * hb + h) * blk, blk), blk)
-            t_down[:, :, :, at] = shaped(dot(hid_t[h], gs[s, home_h]))
-
-    scatter_step(2, 0)
+            t_all[:, :, :, at] = shaped(dot(xt[s, home_h], gp[h]))
+            at = pl.ds(pl.multiple_of(downs + (s * hb + h) * blk, blk), blk)
+            t_all[:, :, :, at] = shaped(dot(hid_t[h], gs[s, home_h]))
+
+    rank_in_t = rank_in.T
+    rank_back_t = rank_back.T
+    for j in range(hb):
+        at = slice(j * blk, (j + 1) * blk)
+        t_all[:, :, :, ranks + j * blk : ranks + (j + 1) * blk] = shaped(
+            dot(rank_in_t, grad_all[:, at]) + dot(rank_back_t, hidden_all[:, at])
+        )
+    scatter_step(0)
 
     def side_pass(i):
         tensor, b = sides[i]
@@ -519,19 +610,9 @@
         side_mid[tensor, b] = (side_mid[tensor, b].astype(F32) + own).astype(BF16)
         side_copy(i, 1).start()
 
-    rank_in_t = rank_in.T
-    rank_back_t = rank_back.T
-    for j in range(hb):
-        at = slice(j * blk, (j + 1) * blk)
-        t_low[:, :, :, at] = shaped(
-            dot(rank_in_t, grad_all[:, at]) + dot(rank_back_t, hidden_all[:, at])
-        )
-    scatter_step(1, 1)
     two.middle()
+    scatter_step(1)
     side_pass(0)
-    scatter_step(2, 1)
-    scatter_step(1, 2)
-    side_pass(1)
     two.end()
     rank2 = rank_two[...].reshape(tokens, blk)
     rank_grad = jnp.where(is_low, rank2, zero)
@@ -540,53 +621,50 @@
     rank_mid_t = rank_mid.T
     for j in range(2):
         at = slice(j * blk, (j + 1) * blk)
-        to = slice(hidden_dev + j * blk, hidden_dev + (j + 1) * blk)
-        t_low[:, :, :, to] = shaped(
-            dot(rank_grad_t, x_ref[:, at]) + dot(rank_mid_t, g_ref[:, at])
-        )
-    scatter_step(0, 0)
-    scatter_step(2, 2)
-    scatter_step(1, 3)
-    scatter_step(0, 1)
-    side_pass(2)
-    for k in range(3, rounds + 1):
-        scatter_step(2, k)
-        if k + 1 <= rounds:
-            scatter_step(1, k + 1)
-        scatter_step(0, k - 1)
-        if k == 3:
-            side_pass(3)
-    scatter_step(0, rounds)
-
-    for i, (tensor, b) in enumerate(sides):
+        t_low[:, :, :, at] = shaped(dot(rank_grad_t, x_ref[:, at]) + dot(rank_mid_t, g_ref[:, at]))
+    low_scatter.begin(0)
+
+    def result(i):
+        tensor, b = sides[i]
         at = slice(b * blk, (b + 1) * blk)
-        to = slice(hidden_dev + b * blk, hidden_dev + (b + 1) * blk)
         rank = rank_mid if tensor == 0 else rank_grad
-        total = side(tensor, 0, b) + dot(rank, m_low[:, to])
+        total = side(tensor, 0, b) + dot(rank, m_two[:, at])
         side_copy(i, 1).wait_recv()
         total = total + side_end[tensor, b].astype(F32)
         ref = out_ref if tensor == 0 else ig_ref
         ref[:, at] = total.astype(BF16)
 
-    def whole(i):
-        return jnp.concatenate([one_chunk.result for one_chunk in scatters[i]], axis=1)
-
-    for i, ref in ((1, gbu_ref), (2, gbd_ref)):
-        total = whole(i).astype(BF16)
+    scatter_step(2)
+    side_pass(1)
+    scatter_step(3)
+    side_pass(2)
+    low_scatter.wait(0)
+    low_scatter.begin(1)
+    result(0)
+    scatter_step(4)
+    side_pass(3)
+    result(1)
+    scatter_step(5)
+    low_scatter.wait(1)
+    low = low_scatter.result
+    gul_ref[...] = low[:half].astype(BF16)
+    gdr_ref[...] = low[half:].astype(BF16)
+    result(2)
+    for k in range(6, rounds + 1):
+        scatter_step(k)
+    result(3)
+
+    total = jnp.concatenate([one_chunk.result for one_chunk in scatters], axis=1)
+    for first, ref in ((0, gbu_ref), (downs, gbd_ref)):
         for s in range(SLOTS):
             for h in range(hb):
-                at = (s * hb + h) * blk
-                ref[h, s] = total[:, at : at + blk]
-    low = whole(0)
-    gur_ref[...] = low[:half, :hidden_dev].astype(BF16)
-    gdl_ref[...] = low[half:, :hidden_dev].astype(BF16)
-    gul_ref[...] = low[:half, hidden_dev:].astype(BF16)
-    gdr_ref[...] = low[half:, hidden_dev:].astype(BF16)
-
-    for i in range(3):
-        for kind in range(4):
-            gathers[i][kind].finish()
-            scatters[i][kind].finish()
+                at = first + (s * hb + h) * blk
+                ref[h, s] = total[:, at : at + blk].astype(BF16)
+    gur_ref[...] = total[:half, ranks:].astype(BF16)
+    gdl_ref[...] = total[half:, ranks:].astype(BF16)
+
+    for one_chunk in gathers + scatters + [low_gather, low_scatter]:
+        one_chunk.finish()
     for i in range(8):
         y_copy(i, 0).wait_send()
         y_copy(i, 1).wait_send()
@@ -597,6 +675,12 @@
     two.finish()
 
 
+def hand_over(*refs):
+    n = len(refs) // 2
+    for source, target in zip(refs[:n], refs[n:]):
+        target[...] = source[...]
+
+
 def per_device(
     nx, nz, nh,
     inputs, out_grad, home_block, blocks_up, blocks_down, up_left, up_right, down_left, down_right,
@@ -605,23 +689,23 @@
     hb, slots, rows, blk = blocks_up.shape
     hidden_dev = hb * blk
     scale = float(nx * nz * tokens) ** (-0.5)
-    low_cols, blk_cols = hidden_dev + width_dev, slots * hb * blk
+    all_cols = 2 * slots * hb * blk + hidden_dev
     vmem = pl.BlockSpec(memory_space=pltpu.VMEM)
     smem = pl.BlockSpec(memory_space=pltpu.SMEM)
 
     def buf(shape, dtype=BF16):
         return pltpu.VMEM(shape, dtype)
 
-    gathered = [buf((nx, nz, rows, c)) for c in (low_cols, blk_cols, blk_cols)]
-    landing = []
-    for c in (low_cols, blk_cols, blk_cols):
-        w = c // 4
-        landing += [
-            buf((2, nz - 1, nx, rows, w)),
-            buf((2, nx - 1, rows, w)),
-            buf((2, nx - 1, nz, rows, w)),
-            buf((2, nz - 1, rows, w)),
-        ]
+    gathered = [buf((nx, nz, rows, c)) for c in (width_dev, all_cols)]
+    w = all_cols // 4
+    landing = [
+        buf((nz, nx, rows, width_dev)),
+        buf((nx, rows, width_dev)),
+        buf((2, nz - 1, nx, rows, w)),
+        buf((2, nx - 1, rows, w)),
+        buf((2, nx - 1, nz, rows, w)),
+        buf((2, nz - 1, rows, w)),
+    ]
     ups = up_left.T, down_left.T
     outs = pl.pallas_call(
         functools.partial(layer, nx, nz, nh, scale),
@@ -639,12 +723,11 @@
         + [
             buf((slots, blk, hidden_dev)),
             buf((slots, hidden_dev, blk)),
-            buf((blk, low_cols)),
+            buf((blk, hidden_dev)),
+            buf((blk, width_dev)),
             buf((slots, 2, tokens, blk)),
             buf((slots, 2, tokens, blk)),
             buf((slots, 2, blk, tokens)),
-            buf((8, 128), F32),
-            buf((8, 128), F32),
             buf((hb, blk, tokens)),
             buf((hb, tokens, blk)),
             buf((2, tokens, hidden_dev)),
@@ -656,11 +739,12 @@
             buf((2, 2, tokens, blk)),
             buf((2, 2, tokens, blk)),
             buf((2, 2, tokens, blk)),
-            pltpu.SemaphoreType.DMA((3, 4, 4)),
-            pltpu.SemaphoreType.DMA((3, 4, nx + nz - 2)),
-            pltpu.SemaphoreType.DMA((3, 4, 4)),
-            pltpu.SemaphoreType.DMA((3, 4, nx + nz - 2)),
+            pltpu.SemaphoreType.DMA((2, max(nx, nz) * (min(nx, nz) + 1))),
+            pltpu.SemaphoreType.DMA((2, max(nx, nz) * (min(nx, nz) + 1))),
+            pltpu.SemaphoreType.DMA((4, 4)),
+            pltpu.SemaphoreType.DMA((4, nx + nz - 2)),
             pltpu.SemaphoreType.DMA((2, 4, nh)),
+            pltpu.SemaphoreType.DMA((2, 2, 2, max(nx, nz))),
             pltpu.SemaphoreType.DMA((4, 2, 8)),
         ],
         compiler_params=pltpu.CompilerParams(
@@ -669,7 +753,12 @@
     )(
         inputs, out_grad, home_block, blocks_up, blocks_down, ups[0], up_right, ups[1], down_right,
     )
-    out, ig, gbu, gbd, gul, gur, gdl, gdr = outs
+    out, ig, gbu, gbd, gul, gur, gdl, gdr = pl.pallas_call(
+        hand_over,
+        out_shape=[jax.ShapeDtypeStruct(a.shape, a.dtype) for a in outs],
+        in_specs=[vmem] * len(outs),
+        out_specs=[vmem] * len(outs),
+    )(*outs)
     return out, ig, gbu, gbd, gul.T, gur, gdl.T, gdr
 
 

time: 148 us -> 128 us (0.86); the launches traced: 145 us -> 128 us
  Pallas kernels: 138 us -> 127 us
  local copies, waits for them, and re-layouts: 6.67 us -> 0 us
    pallas_call x1, Pallas kernels: 138 us -> 125 us  [per_device(): pl.pallas_call(functools.partial(layer, nx, nz, nh, scale), out_shape=[ja...]
    unnamed x22 -> x0, local copies, waits for them, and re-layouts: 6.67 us -> none
    pallas_call x0 -> x1, Pallas kernels: none -> 1.92 us  [per_device(): pl.pallas_call(hand_over, out_shape=[jax.ShapeDtypeStruct(a.shape, a.dtyp...]
where the time goes in v2:
time: 128 us
  Pallas kernels  127 us (99%)
    pallas_call x1, Pallas kernels, per_device(): pl.pallas_call(functools.partial(layer, nx, nz, nh, scale), out_shape=[ja...  125 us

profile of v2, /device:TPU:1, one launch (start us, length us, event | category | flops | bytes accessed | tf_op | source)
XLA Modules:
  0.0 127.9 jit_solution(7929735767021035753)
XLA Ops:
  0.6 125.4 %shard_map.152 = (bf16[256,512]{1,0:T(8,128)(2,1)}, bf16[256,512]{1,0:T(8,128)(2,1)}, bf16[4,3,8,256]{3,2,1,0:T(8,128)(2,1)}, bf16[4,3,8,256]{3,2,1,0:T(8,128)(2...) custom-call(bf16[256,512]{1,0:T(8,128)(2,1)} %x_ref.1, ...), custom_call_target="tpu_custom_call" | custom-call | tf_op jit(solution)/shard_map/pallas_call | solution.py:710
  126.0 1.9 %shard_map.153 = (bf16[256,512]{1,0:T(8,128)(2,1)}, bf16[256,512]{1,0:T(8,128)(2,1)}, bf16[4,3,8,256]{3,2,1,0:T(8,128)(2,1)}, bf16[4,3,8,256]{3,2,1,0:T(8,128)(2...) custom-call(bf16[256,512]{1,0:T(8,128)(2,1)} %get-tuple-element.24.ref, ...), custom_call_target="tpu_custom_call" | custom-call | tf_op jit(solution)/shard_map/pallas_call | solution.py:756

commit v3 on v2

--- a/solution.py
+++ b/solution.py
@@ -68,10 +68,15 @@
     return [(0, n // 2)] + ([(1, n // 2 - 1)] if n > 2 else [])
 
 
+def scatter_widths(total):
+    return [11 * total // 56] * 2 + [17 * total // 56] * 2
+
+
 class TorusGather:
     def __init__(self, place, buf, kind, send_sem, recv_sem):
         self.place, self.buf, self.kind = place, buf, kind
-        self.width = buf.shape[3] // 2
+        total = buf.shape[3]
+        self.first, self.width = ((0, 11 * total // 28), (11 * total // 28, 17 * total // 28))[kind]
         self.axes = ("x", "z") if kind == 0 else ("z", "x")
         self.n = [place.size[a] for a in self.axes]
         self.send_sem, self.recv_sem = send_sem, recv_sem
@@ -84,8 +89,7 @@
         at = {}
         for axis, n, off in zip(self.axes, self.n, (f, g)):
             at[axis] = wrap(self.place.pos[axis] - off, n)
-        first = self.kind * self.width
-        width = self.width
+        first, width = self.first, self.width
         if part is not None:
             width = width // 2
             first = first + part * width
@@ -151,9 +155,10 @@
 
 
 class Scatter:
-    def __init__(self, place, terms, kind, width, first_buf, second_buf, send_sem, recv_sem):
+    def __init__(self, place, terms, kind, widths, first_buf, second_buf, send_sem, recv_sem):
         self.place, self.terms, self.kind = place, terms, kind
-        self.columns = pl.ds(kind * width, width)
+        first = sum(widths[:kind])
+        self.columns = pl.ds(first, widths[kind])
         self.bufs = (first_buf, second_buf)
         self.send_sem, self.recv_sem = send_sem, recv_sem
         self.axes = gather_axes(kind)[::-1]
@@ -475,38 +480,37 @@
         rank_parts[index] = mixed.astype(BF16)
         which.start()
 
+    def exchange(begun, passed):
+        for i in begun:
+            y_copy(i, 0).start()
+        for i in passed:
+            pass_on(i)
+
     low_gather.begin(0)
     gather_step(0)
-    for i in range(4):
-        y_copy(i, 0).start()
+    exchange((0, 1), ())
     low_gather.wait(0)
     low_gather.begin(1)
     gather_step(1)
-    for i in range(4, 8):
-        y_copy(i, 0).start()
-    pass_on(0)
+    exchange((2, 3), (0,))
     gather_step(2)
+    exchange((4, 5), (1, 2))
     low_gather.wait(1)
     for j in range(2):
         m_two[:, j * blk : (j + 1) * blk] = flat(g_low, j * blk, blk)
     rank_start(one, 0, dot(x_ref[...], m_two[...], NT), dot(g_ref[...], m_two[...], NT))
-    pass_on(1)
-    pass_on(2)
     gather_step(3)
-    pass_on(3)
-    pass_on(4)
+    exchange((6, 7), (3, 4))
     gather_step(4)
+    exchange((), (5, 6))
     one.middle()
-    pass_on(5)
     gather_step(5)
-    pass_on(6)
-    pass_on(7)
+    exchange((), (7,))
     for i in range(4):
         y_copy(i, 1).wait_recv()
     for s in range(SLOTS):
         for b in range(2):
             xt[s, b] = xs[s, b].T
-    one.end()
     for k in range(6, rounds + 1):
         gather_step(k)
     for j in range(SLOTS * hb):
@@ -516,6 +520,7 @@
         m_one[:, j * blk : (j + 1) * blk] = flat(g_all, ranks + j * blk, blk)
     for i in range(4, 8):
         y_copy(i, 1).wait_recv()
+    one.end()
 
     rank1 = rank_one[...].reshape(tokens, blk)
     zero = jnp.zeros_like(rank1)
@@ -564,13 +569,18 @@
     rank_start(
         two, 1, dot(grad_all, m_one[...], NT), dot(hidden_all, m_one[...], NT)
     )
-    for i, (tensor, b) in enumerate(sides):
+
+    def side_begin(i):
+        tensor, b = sides[i]
         side_send[tensor, b] = side(tensor, 1, b).astype(BF16)
         side_copy(i, 0).start()
 
+    for i in range(2):
+        side_begin(i)
+
     scatters = [
         Scatter(
-            place, t_all, kind, t_all.shape[3] // 4,
+            place, t_all, kind, scatter_widths(t_all.shape[3]),
             *((all_z1, all_x2) if kind < 2 else (all_x1, all_z2)),
             rs_send, rs_recv,
         )
@@ -610,9 +620,13 @@
         side_mid[tensor, b] = (side_mid[tensor, b].astype(F32) + own).astype(BF16)
         side_copy(i, 1).start()
 
+    scatter_step(1)
+    side_begin(2)
     two.middle()
-    scatter_step(1)
     side_pass(0)
+    scatter_step(2)
+    side_begin(3)
+    side_pass(1)
     two.end()
     rank2 = rank_two[...].reshape(tokens, blk)
     rank_grad = jnp.where(is_low, rank2, zero)
@@ -634,15 +648,13 @@
         ref = out_ref if tensor == 0 else ig_ref
         ref[:, at] = total.astype(BF16)
 
-    scatter_step(2)
-    side_pass(1)
     scatter_step(3)
     side_pass(2)
+    scatter_step(4)
     low_scatter.wait(0)
     low_scatter.begin(1)
+    side_pass(3)
     result(0)
-    scatter_step(4)
-    side_pass(3)
     result(1)
     scatter_step(5)
     low_scatter.wait(1)
@@ -697,14 +709,14 @@
         return pltpu.VMEM(shape, dtype)
 
     gathered = [buf((nx, nz, rows, c)) for c in (width_dev, all_cols)]
-    w = all_cols // 4
+    w_z, w_x = scatter_widths(all_cols)[0], scatter_widths(all_cols)[3]
     landing = [
         buf((nz, nx, rows, width_dev)),
         buf((nx, rows, width_dev)),
-        buf((2, nz - 1, nx, rows, w)),
-        buf((2, nx - 1, rows, w)),
-        buf((2, nx - 1, nz, rows, w)),
-        buf((2, nz - 1, rows, w)),
+        buf((2, nz - 1, nx, rows, w_z)),
+        buf((2, nx - 1, rows, w_z)),
+        buf((2, nx - 1, nz, rows, w_x)),
+        buf((2, nz - 1, rows, w_x)),
     ]
     ups = up_left.T, down_left.T
     outs = pl.pallas_call(

time: 128 us -> 118 us (0.922)
  Pallas kernels: 127 us -> 117 us
    pallas_call x1, Pallas kernels: 125 us -> 115 us  [per_device(): pl.pallas_call(functools.partial(layer, nx, nz, nh, scale), out_shape=[ja...]
where the time goes in v3:
time: 118 us; the launch traced here: 117 us
  Pallas kernels  117 us (99%)
    pallas_call x1, Pallas kernels, per_device(): pl.pallas_call(functools.partial(layer, nx, nz, nh, scale), out_shape=[ja...  115 us

profile of v3, /device:TPU:1, one launch (start us, length us, event | category | flops | bytes accessed | tf_op | source)
XLA Modules:
  0.0 117.5 jit_solution(4995588251186889934)
XLA Ops:
  0.6 114.9 %shard_map.152 = (bf16[256,512]{1,0:T(8,128)(2,1)}, bf16[256,512]{1,0:T(8,128)(2,1)}, bf16[4,3,8,256]{3,2,1,0:T(8,128)(2,1)}, bf16[4,3,8,256]{3,2,1,0:T(8,128)(2...) custom-call(bf16[256,512]{1,0:T(8,128)(2,1)} %x_ref.1, ...), custom_call_target="tpu_custom_call" | custom-call | tf_op jit(solution)/shard_map/pallas_call | solution.py:722
  115.5 1.9 %shard_map.153 = (bf16[256,512]{1,0:T(8,128)(2,1)}, bf16[256,512]{1,0:T(8,128)(2,1)}, bf16[4,3,8,256]{3,2,1,0:T(8,128)(2,1)}, bf16[4,3,8,256]{3,2,1,0:T(8,128)(2...) custom-call(bf16[256,512]{1,0:T(8,128)(2,1)} %get-tuple-element.24.ref, ...), custom_call_target="tpu_custom_call" | custom-call | tf_op jit(solution)/shard_map/pallas_call | solution.py:768

commit v4 on v3

--- a/solution.py
+++ b/solution.py
@@ -622,11 +622,12 @@
 
     scatter_step(1)
     side_begin(2)
+    side_pass(0)
     two.middle()
-    side_pass(0)
     scatter_step(2)
     side_begin(3)
     side_pass(1)
+    scatter_step(3)
     two.end()
     rank2 = rank_two[...].reshape(tokens, blk)
     rank_grad = jnp.where(is_low, rank2, zero)
@@ -648,22 +649,21 @@
         ref = out_ref if tensor == 0 else ig_ref
         ref[:, at] = total.astype(BF16)
 
-    scatter_step(3)
     side_pass(2)
     scatter_step(4)
+    side_pass(3)
     low_scatter.wait(0)
     low_scatter.begin(1)
-    side_pass(3)
     result(0)
     result(1)
     scatter_step(5)
+    result(2)
+    for k in range(6, rounds + 1):
+        scatter_step(k)
     low_scatter.wait(1)
     low = low_scatter.result
     gul_ref[...] = low[:half].astype(BF16)
     gdr_ref[...] = low[half:].astype(BF16)
-    result(2)
-    for k in range(6, rounds + 1):
-        scatter_step(k)
     result(3)
 
     total = jnp.concatenate([one_chunk.result for one_chunk in scatters], axis=1)

time: 118 us -> 114 us (0.966)
  Pallas kernels: 117 us -> 114 us
    pallas_call x1, Pallas kernels: 115 us -> 112 us  [per_device(): pl.pallas_call(functools.partial(layer, nx, nz, nh, scale), out_shape=[ja...]
where the time goes in v4:
time: 114 us
  Pallas kernels  114 us (100%)
    pallas_call x1, Pallas kernels, per_device(): pl.pallas_call(functools.partial(layer, nx, nz, nh, scale), out_shape=[ja...  112 us

profile of v4, /device:TPU:1, one launch (start us, length us, event | category | flops | bytes accessed | tf_op | source)
XLA Modules:
  0.0 114.3 jit_solution(10114331427356973314)
XLA Ops:
  0.6 111.7 %shard_map.152 = (bf16[256,512]{1,0:T(8,128)(2,1)}, bf16[256,512]{1,0:T(8,128)(2,1)}, bf16[4,3,8,256]{3,2,1,0:T(8,128)(2,1)}, bf16[4,3,8,256]{3,2,1,0:T(8,128)(2...) custom-call(bf16[256,512]{1,0:T(8,128)(2,1)} %x_ref.1, ...), custom_call_target="tpu_custom_call" | custom-call | tf_op jit(solution)/shard_map/pallas_call | solution.py:722
  112.4 1.9 %shard_map.153 = (bf16[256,512]{1,0:T(8,128)(2,1)}, bf16[256,512]{1,0:T(8,128)(2,1)}, bf16[4,3,8,256]{3,2,1,0:T(8,128)(2,1)}, bf16[4,3,8,256]{3,2,1,0:T(8,128)(2...) custom-call(bf16[256,512]{1,0:T(8,128)(2,1)} %get-tuple-element.24.ref, ...), custom_call_target="tpu_custom_call" | custom-call | tf_op jit(solution)/shard_map/pallas_call | solution.py:768

commit v5 on v4

--- a/solution.py
+++ b/solution.py
@@ -401,7 +401,7 @@
     out_ref, ig_ref, gbu_ref, gbd_ref, gul_ref, gur_ref, gdl_ref, gdr_ref,
     g_low, g_all, t_low, t_all,
     low_first, low_second, all_z1, all_x2, all_x1, all_z2,
-    w_up, w_down, m_one, m_two, xs, gs, xt, hid_t, gp, hid_m, gp_m,
+    w_up, w_down, m_one, m_two, xs, gs, xt, own_sum, hid_t, gp, hid_m, gp_m,
     rank_parts, rank_got, rank_one, rank_two,
     side_send, side_mid, side_end,
     ag_send, ag_recv, rs_send, rs_recv, rank_sems, low_sems, y_sems,
@@ -639,11 +639,16 @@
         t_low[:, :, :, at] = shaped(dot(rank_grad_t, x_ref[:, at]) + dot(rank_mid_t, g_ref[:, at]))
     low_scatter.begin(0)
 
+    def own_part(i):
+        tensor, b = sides[i]
+        at = slice(b * blk, (b + 1) * blk)
+        rank = rank_mid if tensor == 0 else rank_grad
+        own_sum[i] = side(tensor, 0, b) + dot(rank, m_two[:, at])
+
     def result(i):
         tensor, b = sides[i]
         at = slice(b * blk, (b + 1) * blk)
-        rank = rank_mid if tensor == 0 else rank_grad
-        total = side(tensor, 0, b) + dot(rank, m_two[:, at])
+        total = own_sum[i]
         side_copy(i, 1).wait_recv()
         total = total + side_end[tensor, b].astype(F32)
         ref = out_ref if tensor == 0 else ig_ref
@@ -654,6 +659,8 @@
     side_pass(3)
     low_scatter.wait(0)
     low_scatter.begin(1)
+    for i in range(4):
+        own_part(i)
     result(0)
     result(1)
     scatter_step(5)
@@ -740,6 +747,7 @@
             buf((slots, 2, tokens, blk)),
             buf((slots, 2, tokens, blk)),
             buf((slots, 2, blk, tokens)),
+            buf((4, tokens, blk), F32),
             buf((hb, blk, tokens)),
             buf((hb, tokens, blk)),
             buf((2, tokens, hidden_dev)),

time: 114 us -> 114 us (level)
  no operation moved by 1% of the time
where the time goes in v5:
time: 114 us
  Pallas kernels  114 us (100%)
    pallas_call x1, Pallas kernels, per_device(): pl.pallas_call(functools.partial(layer, nx, nz, nh, scale), out_shape=[ja...  112 us

profile of v5, /device:TPU:1, one launch (start us, length us, event | category | flops | bytes accessed | tf_op | source)
XLA Modules:
  0.0 114.3 jit_solution(2027381898504617263)
XLA Ops:
  0.6 111.7 %shard_map.152 = (bf16[256,512]{1,0:T(8,128)(2,1)}, bf16[256,512]{1,0:T(8,128)(2,1)}, bf16[4,3,8,256]{3,2,1,0:T(8,128)(2,1)}, bf16[4,3,8,256]{3,2,1,0:T(8,128)(2...) custom-call(bf16[256,512]{1,0:T(8,128)(2,1)} %x_ref.1, ...), custom_call_target="tpu_custom_call" | custom-call | tf_op jit(solution)/shard_map/pallas_call | solution.py:729
  112.4 1.9 %shard_map.153 = (bf16[256,512]{1,0:T(8,128)(2,1)}, bf16[256,512]{1,0:T(8,128)(2,1)}, bf16[4,3,8,256]{3,2,1,0:T(8,128)(2,1)}, bf16[4,3,8,256]{3,2,1,0:T(8,128)(2...) custom-call(bf16[256,512]{1,0:T(8,128)(2,1)} %get-tuple-element.24.ref, ...), custom_call_target="tpu_custom_call" | custom-call | tf_op jit(solution)/shard_map/pallas_call | solution.py:776
